TPU v7x, 128 devices: a whole 4x4x4 slice. The times are simulated.
128 devices in a mesh: gx: 32 (over z, x, core), gy: 4 (over y).
Axes of the slice: x: 4, y: 4, z: 4, core: 2. Of those that a mesh axis runs over, the one named last changes fastest.
Arguments:
- misfit: float32 [131072, 2, 256], P(('gx', 'gy')), may hold values from -6 to 6
- owners: int32 [131072], P(('gx', 'gy')), may hold values from 0 to 127, as said below
- offsets: int32 [131072], P(('gx', 'gy')), may hold values from 0 to 130816, as said below
- counts: int32 [128], P(('gx', 'gy')), may hold values from 640 to 1024
- viscosity: float32 [1024, 16384], P('gy', 'gx'), may hold values from 0.05 to 0.5
- friction: float32 [1024, 16384], P('gy', 'gx'), may hold values from 0.2 to 2
Outputs:
- adjoint_field: float32 [2, 1024, 16384], P(None, 'gy', 'gx')
- residual: float32 [2, 1024, 16384], P(None, 'gy', 'gx')
Inputs may be any that keep to these rules, and one draw needn't show every extreme that they name: `owners`: within the slots of one device no owner is named more than 8 times; the first 8 slots of every device name one common owner, drawn from the seed. `offsets`: A segment's 256 pixels stay in one row of its owner's block.
All inputs are finite; a program needn't handle non-finite values.
Results may differ from a plain program's by a relative error of at most 0.00021.
Values sent between devices are 32-bit elements; how exact they have to be, the bound alone decides.
A program may use at most 64 MiB of HBM per device.

v0:
```python
import jax
import jax.numpy as jnp
from jax import lax
from jax.sharding import PartitionSpec as P

PAIR_CAP = 8
ITERS = 3


def with_halo(block, sides, width):
    for axis, dim in sides:
        count = lax.axis_size(axis)
        forward = [(i, i + 1) for i in range(count - 1)]
        backward = [(target, source) for source, target in forward]
        low = lax.ppermute(
            lax.slice_in_dim(block, block.shape[dim] - width, None, axis=dim), axis, forward
        )
        high = lax.ppermute(lax.slice_in_dim(block, 0, width, axis=dim), axis, backward)
        block = jnp.concatenate([low, block, high], axis=dim)
    return block


def node_viscosity(padded_eta):
    return 0.25 * (
        padded_eta[:-1, :-1] + padded_eta[1:, :-1] + padded_eta[:-1, 1:] + padded_eta[1:, 1:]
    )


def shelf_operator(padded, node_eta, friction, field):
    pu = padded[0]
    pv = padded[1]
    exx = pu[:-1, 1:] - pu[:-1, :-1]
    eyy = pv[1:, :-1] - pv[:-1, :-1]
    exy = 0.5 * (pu[1:, :-1] - pu[:-1, :-1] + pv[:-1, 1:] - pv[:-1, :-1])
    sxx = node_eta * (4.0 * exx + 2.0 * eyy)
    syy = node_eta * (2.0 * exx + 4.0 * eyy)
    sxy = 4.0 * node_eta * exy
    image_u = sxx[1:, :-1] - sxx[1:, 1:] + 0.5 * (sxy[:-1, 1:] - sxy[1:, 1:]) + friction * field[0]
    image_v = syy[:-1, 1:] - syy[1:, 1:] + 0.5 * (sxy[1:, :-1] - sxy[1:, 1:]) + friction * field[1]
    return jnp.stack([image_u, image_v])


def shards(misfit, owners, offsets, counts, viscosity, friction):
    count_x = lax.axis_size("gx")
    count_y = lax.axis_size("gy")
    ndev = count_x * count_y
    slots = owners.shape[0]
    pixels = misfit.shape[2]
    rows, columns = viscosity.shape
    capacity = PAIR_CAP
    highest = lax.Precision.HIGHEST
    slot_ids = jnp.arange(slots, dtype=jnp.int32)
    live = slot_ids < counts[0]
    match = (
        (owners[:, None] == jnp.arange(ndev, dtype=jnp.int32)[None, :]) & live[:, None]
    ).astype(jnp.float32)
    lower = (slot_ids[:, None] > slot_ids[None, :]).astype(jnp.float32)
    before = jnp.dot(lower, match, precision=highest, preferred_element_type=jnp.float32)
    rank = jnp.sum(before * match, axis=1).astype(jnp.int32)
    target = jnp.where(live, owners * capacity + rank, ndev * capacity)
    place_bool = target[None, :] == jnp.arange(ndev * capacity, dtype=jnp.int32)[:, None]
    placement = place_bool.astype(jnp.float32)
    send_values = jnp.dot(
        placement,
        misfit.reshape(slots, 2 * pixels),
        precision=highest,
        preferred_element_type=jnp.float32,
    )
    send_starts = jnp.sum(jnp.where(place_bool, offsets[None, :], 0), axis=1)
    got_values, got_starts = (
        lax.all_to_all(
            send_values.reshape(ndev, capacity, 2 * pixels),
            ("gx", "gy"),
            split_axis=0,
            concat_axis=0,
            tiled=True,
        ),
        lax.all_to_all(
            send_starts.reshape(ndev, capacity),
            ("gx", "gy"),
            split_axis=0,
            concat_axis=0,
            tiled=True,
        ),
    )
    received = ndev * capacity
    block = 64
    blocks = received // block
    got_values = got_values.reshape(blocks, block, 2, pixels)
    got_starts = got_starts.reshape(blocks, block)
    column_ids = jnp.arange(columns, dtype=jnp.int32)
    pixel_ids = jnp.arange(pixels, dtype=jnp.int32)
    row_ids = jnp.arange(rows, dtype=jnp.int32)

    def deposit(total, items):
        values, starts = items
        row_of = starts // columns
        column_of = starts % columns
        spread = (
            column_ids[None, None, :] == column_of[:, None, None] + pixel_ids[None, :, None]
        ).astype(jnp.float32)
        placed = jnp.einsum("kcp,kpx->kcx", values, spread, precision=highest)
        row_hot = (row_of[:, None] == row_ids[None, :]).astype(jnp.float32)
        return (total + jnp.einsum("kr,kcx->crx", row_hot, placed, precision=highest), None)

    rhs, unused = lax.scan(
        deposit, jnp.zeros((2, rows, columns), jnp.float32), (got_values, got_starts)
    )
    padded_eta = with_halo(viscosity, (("gx", 1), ("gy", 0)), 1)
    node_eta = node_viscosity(padded_eta)

    def squares(values):
        return lax.psum(jnp.sum(values * values), ("gx", "gy"))

    adjoint_field = jnp.zeros_like(rhs)
    residual = rhs
    direction = rhs
    norm_now = squares(residual)
    for step in range(ITERS):
        padded = with_halo(direction, (("gx", 2), ("gy", 1)), 1)
        image = shelf_operator(padded, node_eta, friction, direction)
        alpha = norm_now / lax.psum(jnp.sum(direction * image), ("gx", "gy"))
        adjoint_field = adjoint_field + alpha * direction
        residual = residual - alpha * image
        norm_next = squares(residual)
        direction = residual + norm_next / norm_now * direction
        norm_now = norm_next
    return (adjoint_field, residual)


def solution(mesh):
    in_specs = (
        P(("gx", "gy"), None, None),
        P(("gx", "gy")),
        P(("gx", "gy")),
        P(("gx", "gy")),
        P("gy", "gx"),
        P("gy", "gx"),
    )
    out_specs = (P(None, "gy", "gx"), P(None, "gy", "gx"))
    return jax.shard_map(shards, mesh=mesh, in_specs=in_specs, out_specs=out_specs, check_vma=False)
```

profile of v0, /device:TPU:1, one launch (start us, length us, event | category | flops | bytes accessed | tf_op | source)
XLA Modules:
  0.0 699.0 jit_solution(13530762765625329876)
XLA Ops:
  4.1 11.5 %all-to-all-start.1 = ((s32[128,1,8]{2,1,0:T(1,128)}), s32[128,1,8]{2,1,0:T(1,128)S(1)}, u32[]{:S(2)}, u32[]{:S(2)}) async-start(s32[128,1,8]{2,1,0:T(1,128)} %bitcast.1), calls=%async_computation.1 | async-start | bytes 131072 | tf_op jit(solution)/shard_map/all_to_all | solution.py:78
  41.6 17.7 %collective-permute-done = f32[256,1]{1,0:T(8,128)S(1)} collective-permute-done((f32[256,1]{1,0:T(8,128)S(1)}, f32[256,1]{1,0:T(8,128)S(1)}, u32[]{:S(2)}, u32[]{:S(2)}) %collective-permute-start) | collective-permute-done | bytes 1056 | tf_op jit(solution)/shard_map/ppermute | solution.py:15
  70.9 213.0 %while.15 = (s32[]{:T(128)}, f32[2,256,512]{1,2,0:T(8,128)S(1)}, f32[16,64,2,256]{3,2,1,0:T(2,128)}, s32[16,64]{1,0:T(8,128)S(1)}, s32[]{:T(128)}, /*index=5*/s32[]{:T(128)}) while((s32[]{:T(128)}, f32[2,256,512]{1,2,0:T(8,128)S(1)}, f32[16,64,2,256]{3,2,1,0:T(2,128)}, s32[16,64]{1,0:T(8,128)S(1)}, s32[]{:T(128)}, ...), condition=%wide.region_3.4_spmd.clone.clone, body=%wide.region_2.3_spmd.clone.clone.sunk | while | flops 411600128 | bytes 2885471 | solution.py:106
  71.0 12.2 %fusion.75 = f32[64,2,512]{2,1,0:T(2,128)S(1)} fusion(s32[64,256]{1,0:T(8,128)S(1)} %iota_add_fusion.2, f32[16,64,2,256]{3,2,1,0:T(2,128)} %get-tuple-element.238, s32[]{:T(128)S(6)} %copy.61), kind=kOutput, calls=%fused_computation.3.clone.1 | convolution fusion | flops 209715200 | bytes 458756 | tf_op jit(solution)/shard_map/while/body/eval_jaxpr/kcp,kpx->kcx/dot_general | solution.py:102
  84.3 12.2 %fusion.75 = f32[64,2,512]{2,1,0:T(2,128)S(1)} fusion(s32[64,256]{1,0:T(8,128)S(1)} %iota_add_fusion.2, f32[16,64,2,256]{3,2,1,0:T(2,128)} %get-tuple-element.238, s32[]{:T(128)S(6)} %copy.61), kind=kOutput, calls=%fused_computation.3.clone.1 | convolution fusion | flops 209715200 | bytes 458756 | tf_op jit(solution)/shard_map/while/body/eval_jaxpr/kcp,kpx->kcx/dot_general | solution.py:102
  97.6 12.2 %fusion.75 = f32[64,2,512]{2,1,0:T(2,128)S(1)} fusion(s32[64,256]{1,0:T(8,128)S(1)} %iota_add_fusion.2, f32[16,64,2,256]{3,2,1,0:T(2,128)} %get-tuple-element.238, s32[]{:T(128)S(6)} %copy.61), kind=kOutput, calls=%fused_computation.3.clone.1 | convolution fusion | flops 209715200 | bytes 458756 | tf_op jit(solution)/shard_map/while/body/eval_jaxpr/kcp,kpx->kcx/dot_general | solution.py:102
  110.9 12.2 %fusion.75 = f32[64,2,512]{2,1,0:T(2,128)S(1)} fusion(s32[64,256]{1,0:T(8,128)S(1)} %iota_add_fusion.2, f32[16,64,2,256]{3,2,1,0:T(2,128)} %get-tuple-element.238, s32[]{:T(128)S(6)} %copy.61), kind=kOutput, calls=%fused_computation.3.clone.1 | convolution fusion | flops 209715200 | bytes 458756 | tf_op jit(solution)/shard_map/while/body/eval_jaxpr/kcp,kpx->kcx/dot_general | solution.py:102
  124.2 12.2 %fusion.75 = f32[64,2,512]{2,1,0:T(2,128)S(1)} fusion(s32[64,256]{1,0:T(8,128)S(1)} %iota_add_fusion.2, f32[16,64,2,256]{3,2,1,0:T(2,128)} %get-tuple-element.238, s32[]{:T(128)S(6)} %copy.61), kind=kOutput, calls=%fused_computation.3.clone.1 | convolution fusion | flops 209715200 | bytes 458756 | tf_op jit(solution)/shard_map/while/body/eval_jaxpr/kcp,kpx->kcx/dot_general | solution.py:102
  137.6 12.2 %fusion.75 = f32[64,2,512]{2,1,0:T(2,128)S(1)} fusion(s32[64,256]{1,0:T(8,128)S(1)} %iota_add_fusion.2, f32[16,64,2,256]{3,2,1,0:T(2,128)} %get-tuple-element.238, s32[]{:T(128)S(6)} %copy.61), kind=kOutput, calls=%fused_computation.3.clone.1 | convolution fusion | flops 209715200 | bytes 458756 | tf_op jit(solution)/shard_map/while/body/eval_jaxpr/kcp,kpx->kcx/dot_general | solution.py:102
  150.9 12.2 %fusion.75 = f32[64,2,512]{2,1,0:T(2,128)S(1)} fusion(s32[64,256]{1,0:T(8,128)S(1)} %iota_add_fusion.2, f32[16,64,2,256]{3,2,1,0:T(2,128)} %get-tuple-element.238, s32[]{:T(128)S(6)} %copy.61), kind=kOutput, calls=%fused_computation.3.clone.1 | convolution fusion | flops 209715200 | bytes 458756 | tf_op jit(solution)/shard_map/while/body/eval_jaxpr/kcp,kpx->kcx/dot_general | solution.py:102
  164.2 12.2 %fusion.75 = f32[64,2,512]{2,1,0:T(2,128)S(1)} fusion(s32[64,256]{1,0:T(8,128)S(1)} %iota_add_fusion.2, f32[16,64,2,256]{3,2,1,0:T(2,128)} %get-tuple-element.238, s32[]{:T(128)S(6)} %copy.61), kind=kOutput, calls=%fused_computation.3.clone.1 | convolution fusion | flops 209715200 | bytes 458756 | tf_op jit(solution)/shard_map/while/body/eval_jaxpr/kcp,kpx->kcx/dot_general | solution.py:102
  177.5 12.2 %fusion.75 = f32[64,2,512]{2,1,0:T(2,128)S(1)} fusion(s32[64,256]{1,0:T(8,128)S(1)} %iota_add_fusion.2, f32[16,64,2,256]{3,2,1,0:T(2,128)} %get-tuple-element.238, s32[]{:T(128)S(6)} %copy.61), kind=kOutput, calls=%fused_computation.3.clone.1 | convolution fusion | flops 209715200 | bytes 458756 | tf_op jit(solution)/shard_map/while/body/eval_jaxpr/kcp,kpx->kcx/dot_general | solution.py:102
  190.8 12.2 %fusion.75 = f32[64,2,512]{2,1,0:T(2,128)S(1)} fusion(s32[64,256]{1,0:T(8,128)S(1)} %iota_add_fusion.2, f32[16,64,2,256]{3,2,1,0:T(2,128)} %get-tuple-element.238, s32[]{:T(128)S(6)} %copy.61), kind=kOutput, calls=%fused_computation.3.clone.1 | convolution fusion | flops 209715200 | bytes 458756 | tf_op jit(solution)/shard_map/while/body/eval_jaxpr/kcp,kpx->kcx/dot_general | solution.py:102
  204.1 12.2 %fusion.75 = f32[64,2,512]{2,1,0:T(2,128)S(1)} fusion(s32[64,256]{1,0:T(8,128)S(1)} %iota_add_fusion.2, f32[16,64,2,256]{3,2,1,0:T(2,128)} %get-tuple-element.238, s32[]{:T(128)S(6)} %copy.61), kind=kOutput, calls=%fused_computation.3.clone.1 | convolution fusion | flops 209715200 | bytes 458756 | tf_op jit(solution)/shard_map/while/body/eval_jaxpr/kcp,kpx->kcx/dot_general | solution.py:102
  217.4 12.2 %fusion.75 = f32[64,2,512]{2,1,0:T(2,128)S(1)} fusion(s32[64,256]{1,0:T(8,128)S(1)} %iota_add_fusion.2, f32[16,64,2,256]{3,2,1,0:T(2,128)} %get-tuple-element.238, s32[]{:T(128)S(6)} %copy.61), kind=kOutput, calls=%fused_computation.3.clone.1 | convolution fusion | flops 209715200 | bytes 458756 | tf_op jit(solution)/shard_map/while/body/eval_jaxpr/kcp,kpx->kcx/dot_general | solution.py:102
  230.8 12.2 %fusion.75 = f32[64,2,512]{2,1,0:T(2,128)S(1)} fusion(s32[64,256]{1,0:T(8,128)S(1)} %iota_add_fusion.2, f32[16,64,2,256]{3,2,1,0:T(2,128)} %get-tuple-element.238, s32[]{:T(128)S(6)} %copy.61), kind=kOutput, calls=%fused_computation.3.clone.1 | convolution fusion | flops 209715200 | bytes 458756 | tf_op jit(solution)/shard_map/while/body/eval_jaxpr/kcp,kpx->kcx/dot_general | solution.py:102
  244.1 12.2 %fusion.75 = f32[64,2,512]{2,1,0:T(2,128)S(1)} fusion(s32[64,256]{1,0:T(8,128)S(1)} %iota_add_fusion.2, f32[16,64,2,256]{3,2,1,0:T(2,128)} %get-tuple-element.238, s32[]{:T(128)S(6)} %copy.61), kind=kOutput, calls=%fused_computation.3.clone.1 | convolution fusion | flops 209715200 | bytes 458756 | tf_op jit(solution)/shard_map/while/body/eval_jaxpr/kcp,kpx->kcx/dot_general | solution.py:102
  257.4 12.2 %fusion.75 = f32[64,2,512]{2,1,0:T(2,128)S(1)} fusion(s32[64,256]{1,0:T(8,128)S(1)} %iota_add_fusion.2, f32[16,64,2,256]{3,2,1,0:T(2,128)} %get-tuple-element.238, s32[]{:T(128)S(6)} %copy.61), kind=kOutput, calls=%fused_computation.3.clone.1 | convolution fusion | flops 209715200 | bytes 458756 | tf_op jit(solution)/shard_map/while/body/eval_jaxpr/kcp,kpx->kcx/dot_general | solution.py:102
  270.7 12.2 %fusion.75 = f32[64,2,512]{2,1,0:T(2,128)S(1)} fusion(s32[64,256]{1,0:T(8,128)S(1)} %iota_add_fusion.2, f32[16,64,2,256]{3,2,1,0:T(2,128)} %get-tuple-element.238, s32[]{:T(128)S(6)} %copy.61), kind=kOutput, calls=%fused_computation.3.clone.1 | convolution fusion | flops 209715200 | bytes 458756 | tf_op jit(solution)/shard_map/while/body/eval_jaxpr/kcp,kpx->kcx/dot_general | solution.py:102
  309.4 70.6 %all-reduce = (f32[]{:T(128)}, f32[]{:T(128)}) all-reduce(f32[]{:T(128)} %multiply_reduce_fusion.5, f32[]{:T(128)} %multiply_reduce_fusion.4), channel_id=1, replica_groups=mesh['gx'=32,'gy'=4] {'gx','gy'}, use_global_device_ids=true, to_apply=%region_5.6 | all-reduce | flops 2 | bytes 16 | tf_op jit(solution)/shard_map/psum | solution.py:113
  382.2 63.5 %psum.44 = f32[]{:T(128)} all-reduce(f32[]{:T(128)} %multiply_reduce_fusion.3), channel_id=1, replica_groups=mesh['gx'=32,'gy'=4] {'gx','gy'}, use_global_device_ids=true, to_apply=%region_9.10 | all-reduce | flops 1 | bytes 8 | tf_op jit(solution)/shard_map/psum | solution.py:113
  469.1 66.5 %psum.45 = f32[]{:T(128)} all-reduce(f32[]{:T(128)} %multiply_reduce_fusion.2), channel_id=1, replica_groups=mesh['gx'=32,'gy'=4] {'gx','gy'}, use_global_device_ids=true, to_apply=%region_11.12 | all-reduce | flops 1 | bytes 8 | tf_op jit(solution)/shard_map/psum | solution.py:122
  539.8 62.9 %psum.46 = f32[]{:T(128)} all-reduce(f32[]{:T(128)} %get-tuple-element.151), channel_id=1, replica_groups=mesh['gx'=32,'gy'=4] {'gx','gy'}, use_global_device_ids=true, to_apply=%region_13.14 | all-reduce | flops 1 | bytes 8 | tf_op jit(solution)/shard_map/psum | solution.py:113
  628.1 66.1 %psum.47 = f32[]{:T(128)} all-reduce(f32[]{:T(128)} %multiply_reduce_fusion), channel_id=1, replica_groups=mesh['gx'=32,'gy'=4] {'gx','gy'}, use_global_device_ids=true, to_apply=%region_15.16 | all-reduce | flops 1 | bytes 8 | tf_op jit(solution)/shard_map/psum | solution.py:122
  (172 shorter events, 135.7 us)
Async XLA Ops:
  1.3 1.5 copy-start.11
  1.3 1.5 copy-start.12
  1.3 14.9 %copy-start.9 = (f32[1024,2,256]{2,1,0:T(2,128)S(1)}, f32[1024,2,256]{2,1,0:T(2,128)}, u32[]{:S(2)}) copy-start(f32[1024,2,256]{2,1,0:T(2,128)} %param.8) | copy-start | bytes 6291460
  4.1 21.7 %all-to-all-start.1 = ((s32[128,1,8]{2,1,0:T(1,128)}), s32[128,1,8]{2,1,0:T(1,128)S(1)}, u32[]{:S(2)}, u32[]{:S(2)}) async-start(s32[128,1,8]{2,1,0:T(1,128)} %bitcast.1), calls=%async_computation.1 | async-start | bytes 131072 | tf_op jit(solution)/shard_map/all_to_all | solution.py:78
  25.7 10.2 %copy-start.8 = (f32[256,512]{1,0:T(8,128)S(1)}, f32[256,512]{1,0:T(8,128)}, u32[]{:S(2)}) copy-start(f32[256,512]{1,0:T(8,128)} %param.12) | copy-start | bytes 1572868
  25.7 41.6 %all-to-all-start = ((f32[128,8,512]{2,1,0:T(8,128)}), f32[128,8,512]{2,1,0:T(8,128)}, u32[]{:S(2)}, u32[]{:S(2)}) async-start(f32[128,8,512]{2,1,0:T(8,128)} %fusion.14), calls=%async_computation | async-start | bytes 4194304 | tf_op jit(solution)/shard_map/all_to_all | solution.py:71
  36.1 23.2 %collective-permute-start = (f32[256,1]{1,0:T(8,128)S(1)}, f32[256,1]{1,0:T(8,128)S(1)}, u32[]{:S(2)}, u32[]{:S(2)}) collective-permute-start(f32[256,1]{1,0:T(8,128)S(1)} %get-tuple-element.191), channel_id=1, source_target_pairs={{0,4},{4,8},{8,12},{12,16},{16,20},{20,24},{24,28},{28,32},{32,36}... | collective-permute-start | bytes 3080 | tf_op jit(solution)/shard_map/ppermute | solution.py:15
  39.6 21.8 %collective-permute-start.1 = (f32[256,1]{1,0:T(8,128)S(1)}, f32[256,1]{1,0:T(8,128)S(1)}, u32[]{:S(2)}, u32[]{:S(2)}) collective-permute-start(f32[256,1]{1,0:T(8,128)S(1)} %get-tuple-element.192), channel_id=1, source_target_pairs={{4,0},{8,4},{12,8},{16,12},{20,16},{24,20},{28,24},{32,28},{36,32}... | collective-permute-start | bytes 3080 | tf_op jit(solution)/shard_map/ppermute | solution.py:18
  61.5 9.4 %copy-start.10 = (f32[256,1]{1,0:T(8,128)}, f32[256,1]{1,0:T(8,128)S(1)}, u32[]{:S(2)}) copy-start(f32[256,1]{1,0:T(8,128)S(1)} %collective-permute-done.1) | copy-start | bytes 3076
  61.5 229.8 %collective-permute-start.2 = (f32[1,514]{1,0:T(1,128)S(1)}, f32[1,514]{1,0:T(1,128)S(1)}, u32[]{:S(2)}, u32[]{:S(2)}) collective-permute-start(f32[1,514]{1,0:T(1,128)S(1)} %get-tuple-element.189), channel_id=1, source_target_pairs={{0,1},{1,2},{2,3},{4,5},{5,6},{6,7},{8,9},{9,10},{10,11},{12,13},{... | collective-permute-start | bytes 6176 | tf_op jit(solution)/shard_map/ppermute | solution.py:15
  64.6 226.8 %collective-permute-start.3 = (f32[1,514]{1,0:T(1,128)S(1)}, f32[1,514]{1,0:T(1,128)S(1)}, u32[]{:S(2)}, u32[]{:S(2)}) collective-permute-start(f32[1,514]{1,0:T(1,128)S(1)} %get-tuple-element.190), channel_id=1, source_target_pairs={{1,0},{2,1},{3,2},{5,4},{6,5},{7,6},{9,8},{10,9},{11,10},{13,12},{... | collective-permute-start | bytes 6176 | tf_op jit(solution)/shard_map/ppermute | solution.py:18
  285.6 8.0 %collective-permute-start.5 = (f32[2,256,1]{2,1,0:T(8,128)}, f32[2,256,1]{2,1,0:T(8,128)}, u32[]{:S(2)}, u32[]{:S(2)}) collective-permute-start(f32[2,256,1]{2,1,0:T(8,128)} %copy.43), channel_id=1, source_target_pairs={{4,0},{8,4},{12,8},{16,12},{20,16},{24,20},{28,24},{32,28},{36,32}... | collective-permute-start | bytes 6152 | tf_op jit(solution)/shard_map/ppermute | solution.py:18
  287.5 7.3 %collective-permute-start.4 = (f32[2,256,1]{2,1,0:T(8,128)}, f32[2,256,1]{2,1,0:T(8,128)}, u32[]{:S(2)}, u32[]{:S(2)}) collective-permute-start(f32[2,256,1]{2,1,0:T(8,128)} %copy.42), channel_id=1, source_target_pairs={{0,4},{4,8},{8,12},{12,16},{16,20},{20,24},{24,28},{28,32},{32,36}... | collective-permute-start | bytes 6152 | tf_op jit(solution)/shard_map/ppermute | solution.py:15
  295.6 6.2 collective-permute-start.6
  299.6 4.4 collective-permute-start.7
  306.3 1.3 copy-start.3
  447.4 5.4 collective-permute-start.8
  449.5 7.7 %collective-permute-start.9 = (f32[2,256,1]{2,1,0:T(8,128)S(1)}, f32[2,256,1]{2,1,0:T(8,128)S(1)}, u32[]{:S(2)}, u32[]{:S(2)}) collective-permute-start(f32[2,256,1]{2,1,0:T(8,128)S(1)} %get-tuple-element.184), channel_id=1, source_target_pairs={{4,0},{8,4},{12,8},{16,12},{20,16},{24,20},{28,24},{32,28},{36,32}... | collective-permute-start | bytes 6152 | tf_op jit(solution)/shard_map/ppermute | solution.py:18
  457.3 3.8 collective-permute-start.10
  459.8 4.4 collective-permute-start.11
  605.6 6.8 collective-permute-start.12
  609.2 7.7 %collective-permute-start.13 = (f32[2,256,1]{2,1,0:T(8,128)S(1)}, f32[2,256,1]{2,1,0:T(8,128)S(1)}, u32[]{:S(2)}, u32[]{:S(2)}) collective-permute-start(f32[2,256,1]{2,1,0:T(8,128)S(1)} %get-tuple-element.182), channel_id=1, source_target_pairs={{4,0},{8,4},{12,8},{16,12},{20,16},{24,20},{28,24},{32,28},{36,32}... | collective-permute-start | bytes 6152 | tf_op jit(solution)/shard_map/ppermute | solution.py:18
  616.9 2.7 collective-permute-start.14
  618.4 4.4 collective-permute-start.15
  (7 other events, 6.6 us)
where the time goes:
time: 702 us; the launch traced here: 699 us
  blocking collectives  330 us (47%)
  matrix products  219 us (31%)
  starting transfers between devices  58.8 us (8%)
  waiting for transfers between devices  41 us (6%)
  other arithmetic  26.8 us (4%)
  local copies, waits for them, and re-layouts  15 us (2%)
  between operations  8.13 us (1%)
    psum x3, blocking collectives, squares(): return lax.psum(jnp.sum(values * values), ('gx', 'gy'))  197 us
    dot_general x16, matrix products, deposit(): placed = jnp.einsum('kcp,kpx->kcx', values, spread, precision=highest)  196 us
    psum x2, blocking collectives, shards(): alpha = norm_now / lax.psum(jnp.sum(direction * image), ('gx', 'gy'))  133 us
    ppermute x8, starting transfers between devices, with_halo(): lax.ppermute(lax.slice_in_dim(block, block.shape[dim] - width, None, axis...  23.9 us
    ppermute x8, waiting for transfers between devices, with_halo(): lax.ppermute(lax.slice_in_dim(block, block.shape[dim] - width, None, axis...  21.3 us
    ppermute x8, waiting for transfers between devices, with_halo(): lax.ppermute(lax.slice_in_dim(block, 0, width, axis=dim), axis, backward)  19.7 us
    dot_general x16, matrix products, deposit(): jnp.einsum('kr,kcx->crx', row_hot, placed, precision=highest)  15 us
  transfers between devices with their start and end apart: 18, of which 11 were waited for; matrix products, arithmetic and copies ran while one was open for 33% of the time, Pallas kernels for 0%

commit v1 on v0

v1 whole, which is shorter than its diff:
```python
import functools

import jax
import jax.numpy as jnp
from jax import lax
from jax.experimental import pallas as pl
from jax.experimental.pallas import tpu as pltpu
from jax.sharding import PartitionSpec as P

MESH = pl.DeviceIdType.MESH
CAP = 8
LANES = 128
HALO = 8
MSG = 33
PAD = 40
bf16, f32, i32 = jnp.bfloat16, jnp.float32, jnp.int32


def split3(x):
    hi = x.astype(bf16)
    rest = x - hi.astype(f32)
    mid = rest.astype(bf16)
    low = (rest - mid.astype(f32)).astype(bf16)
    return hi, mid, low


def iota(shape, dim):
    return lax.broadcasted_iota(i32, shape, dim)


def remote(src, dst, send_sem, recv_sem, dev):
    return pltpu.make_async_remote_copy(
        src_ref=src, dst_ref=dst, send_sem=send_sem, recv_sem=recv_sem, device_id=dev, device_id_type=MESH
    )


def kernel(
    n_gx, n_gy, chunk,
    misfit, owners, offsets, counts, viscosity, friction, out_x, out_r,
    parts, send, recv, deposit, field, nodes, q1, q2, q3, strips, halo, sums,
    a2a_send, a2a_recv, self_sem, ex_send, ex_recv, ar_send, ar_recv,
):
    ndev = n_gx * n_gy
    ix, iy = lax.axis_index("gx"), lax.axis_index("gy")
    me = ix * n_gy + iy
    slots = misfit.shape[0] // 4
    rows, columns = viscosity.shape
    chunks = ndev // chunk
    keys = chunk * CAP

    barrier = pltpu.get_barrier_semaphore()

    def greet(p, carry):
        dev = lax.rem(me + p, ndev)
        pl.semaphore_signal(barrier, inc=1, device_id=(dev // n_gy, lax.rem(dev, n_gy)), device_id_type=MESH)
        return carry

    lax.fori_loop(1, ndev, greet, 0)

    count = counts[0]
    lane_blocks = slots // LANES
    upper = (iota((LANES, LANES), 0) < iota((LANES, LANES), 1)).astype(bf16)
    carry = jnp.zeros((ndev, 1), f32)
    hots, targets, weights = [], [], []
    for b in range(lane_blocks):
        own = owners[pl.ds(b, 1), :]
        off = offsets[pl.ds(b, 1), :]
        live = (iota((1, LANES), 1) + b * LANES) < count
        rel = jnp.where(live, lax.rem(own - me + ndev, ndev), -1)
        hot = (iota((ndev, LANES), 0) == rel).astype(f32)
        before = jnp.dot(hot.astype(bf16), upper, preferred_element_type=f32) + carry
        rank = jnp.sum(hot * before, axis=0, keepdims=True).astype(i32)
        carry = carry + jnp.sum(hot, axis=1, keepdims=True)
        targets.append(jnp.where(live, rel * CAP + rank, -1))
        hots.append(hot.astype(bf16))
        mine = lax.rem(iota((LANES, LANES), 0), CAP) == rank
        row_part = jnp.where(mine, lax.shift_right_logical(off, 9).astype(f32), 0.0)
        col_part = jnp.where(mine, lax.bitwise_and(off, 511).astype(f32), 0.0)
        weights.append(jnp.concatenate([row_part, col_part], axis=0).astype(bf16))
    target = jnp.concatenate(targets, axis=1)
    hot = jnp.concatenate(hots, axis=1)
    weight = jnp.concatenate(weights, axis=1)
    meta = lax.dot_general(hot, weight, (((1,), (1,)), ((), ())), preferred_element_type=f32)
    meta = meta[:, :LANES] * 512.0 + meta[:, LANES:]
    send[:, 32, :] = meta

    for t in range(4):
        hi, mid, low = split3(misfit[pl.ds(t, slots, stride=4), :])
        parts[:, pl.ds(t * LANES, LANES)] = hi
        parts[:, pl.ds((4 + t) * LANES, LANES)] = mid
        parts[:, pl.ds((8 + t) * LANES, LANES)] = low

    pl.semaphore_wait(barrier, ndev - 1)

    def pack(g, carry):
        place = ((iota((keys, slots), 0) + g * keys) == target).astype(bf16)
        packed = jnp.dot(place, parts[...], preferred_element_type=f32)
        packed = packed[:, :512] + packed[:, 512:1024] + packed[:, 1024:]
        for t in range(4):
            send[pl.ds(g * chunk, chunk), pl.ds(t * CAP, CAP), :] = packed[:, t * LANES:(t + 1) * LANES].reshape(
                chunk, CAP, LANES
            )

        def push(i, carry):
            p = g * chunk + i
            dev = lax.rem(me + p, ndev)
            remote(
                send.at[p, pl.ds(0, MSG), :], recv.at[p, pl.ds(0, MSG), :], a2a_send.at[g], a2a_recv.at[g],
                (dev // n_gy, lax.rem(dev, n_gy)),
            ).start()
            return carry

        lax.fori_loop(jnp.where(g == 0, 1, 0), chunk, push, 0)
        return carry

    lax.fori_loop(0, chunks, pack, 0)
    own = pltpu.make_async_copy(send.at[0, pl.ds(0, MSG), :], recv.at[0, pl.ds(0, MSG), :], self_sem)
    own.start()

    left, right = lax.rem(ix + n_gx - 1, n_gx), lax.rem(ix + 1, n_gx)
    up, down = lax.rem(iy + n_gy - 1, n_gy), lax.rem(iy + 1, n_gy)
    bottom = HALO + rows
    first, last = pl.ds(0, 8), pl.ds(LANES - 8, 8)
    tile0, tile3 = pl.ds(0, LANES), pl.ds(LANES + rows, LANES)
    part0, part1, whole = pl.ds(0, LANES), pl.ds(rows - LANES, LANES), pl.ds(0, rows)
    lane_tile = iota((8, LANES), 1)
    side = jnp.where(lane_tile < 64, jnp.where(ix < n_gx - 1, 1.0, 0.0), jnp.where(ix > 0, 1.0, 0.0))
    above = jnp.where(iy > 0, 1.0, 0.0)
    below = jnp.where(iy < n_gy - 1, 1.0, 0.0)
    mask_main = jnp.concatenate([jnp.ones((8, columns), f32), side], axis=1)

    def copies(c):
        pair = pl.ds(c, 2)
        main = pl.ds(0, columns)
        moves = (
            (field.at[pair, pl.ds(HALO, 8), main], field.at[pair, pl.ds(bottom, 8), main], (ix, up)),
            (field.at[pair, pl.ds(bottom - 8, 8), main], field.at[pair, pl.ds(0, 8), main], (ix, down)),
            (strips.at[pair, first, whole], halo.at[pair, first, pl.ds(LANES, rows)], (left, iy)),
            (strips.at[pair, last, whole], halo.at[pair, last, pl.ds(LANES, rows)], (right, iy)),
            (strips.at[pair, first, part0], halo.at[pair, first, tile3], (left, up)),
            (strips.at[pair, first, part1], halo.at[pair, first, tile0], (left, down)),
            (strips.at[pair, last, part0], halo.at[pair, last, tile3], (right, up)),
            (strips.at[pair, last, part1], halo.at[pair, last, tile0], (right, down)),
        )
        h = c // 2
        return [remote(s, d, ex_send.at[h, k], ex_recv.at[h, k], dev) for k, (s, d, dev) in enumerate(moves)]

    def offer(c):
        for f in (c, c + 1):
            for j in range(rows // LANES):
                at = pl.ds(HALO + j * LANES, LANES)
                mix = jnp.where(
                    iota((LANES, LANES), 1) < 64, field[f, at, pl.ds(0, LANES)], field[f, at, pl.ds(columns - LANES, LANES)]
                )
                strips[f, :, pl.ds(j * LANES, LANES)] = mix.T
        for copy in copies(c):
            copy.start()

    def accept(c):
        for copy in copies(c):
            copy.wait_recv()
        wrap = pl.ds(columns, LANES)
        main = pl.ds(0, columns)
        for f in (c, c + 1):
            for j in range(rows // LANES):
                turned = halo[f, :, pl.ds((j + 1) * LANES, LANES)].T
                field[f, pl.ds(HALO + j * LANES, LANES), wrap] = turned * side[:1]
            field[f, pl.ds(0, 8), wrap] = halo[f, :, tile0].T[LANES - 8:] * (side * above)
            field[f, pl.ds(bottom, 8), wrap] = halo[f, :, tile3].T[:8] * (side * below)
            field[f, pl.ds(0, 8), main] = field[f, pl.ds(0, 8), main] * above
            field[f, pl.ds(bottom, 8), main] = field[f, pl.ds(bottom, 8), main] * below

    for f in range(4):
        halo[f, pl.ds(8, LANES - 16), :] = jnp.zeros((LANES - 16, halo.shape[2]), f32)
    field[0, pl.ds(HALO, rows), pl.ds(0, columns)] = viscosity[...]
    field[1, pl.ds(HALO, rows), pl.ds(0, columns)] = friction[...]
    offer(0)

    near = min(8, n_gx)
    far = ndev // near

    def stage1(s):
        low, high = lax.rem(ix, near), ix // near * near
        return [
            remote(sums.at[s, 0], sums.at[s, k], ar_send.at[s, k], ar_recv.at[s, k], (high + lax.rem(low + k, near), iy))
            for k in range(1, near)
        ]

    def stage2(s):
        low = lax.rem(ix, near)
        group = ix // near * n_gy + iy
        result = []
        for k in range(1, far):
            other = lax.rem(group + k, far)
            result.append(
                remote(
                    sums.at[s, near], sums.at[s, near + k], ar_send.at[s, near + k], ar_recv.at[s, near + k],
                    (other // n_gy * near + low, lax.rem(other, n_gy)),
                )
            )
        return result

    def add_all(s, terms):
        terms = list(terms) + [jnp.zeros((1, LANES), f32)] * (8 - len(terms))
        sums[s, 0] = jnp.concatenate(terms, axis=0)
        for copy in stage1(s):
            copy.start()
        for copy in stage1(s):
            copy.wait_recv()
        total = sums[s, 0]
        for k in range(1, near):
            total = total + sums[s, k]
        sums[s, near] = total
        for copy in stage2(s):
            copy.start()
        for copy in stage2(s):
            copy.wait_recv()
        total = sums[s, near]
        for k in range(1, far):
            total = total + sums[s, near + k]
        return jnp.sum(total, axis=1, keepdims=True)

    tiles = (rows + 2 * HALO) // 8
    width = columns + LANES

    def east(x):
        return pltpu.roll(x, width - 1, 1)

    def west(x):
        return pltpu.roll(x, 1, 1)

    sub = iota((8, width), 0)

    def south(x, following):
        return pltpu.roll(jnp.where(sub == 0, following, x), 7, 0)

    def north(x, previous):
        return pltpu.roll(jnp.where(sub == 7, previous, x), 1, 0)

    def tile_at(t):
        if isinstance(t, int):
            return pl.ds(t * 8, 8)
        return pl.ds(pl.multiple_of(t * 8, 8), 8)

    accept(0)

    def node_tile(t, total):
        here = field[0, tile_at(t), :]
        following = field[0, tile_at(jnp.minimum(t + 1, tiles - 1)), :]
        pair = here + south(here, following)
        doubled = 0.5 * (pair + east(pair))
        nodes[tile_at(t), :] = doubled
        return total + 5.0 * doubled + field[1, tile_at(t), :]

    total = lax.fori_loop(0, tiles, node_tile, jnp.zeros((8, width), f32))
    total = jnp.sum(total, axis=0, keepdims=True)
    part = sum(total[:, k * LANES:(k + 1) * LANES] for k in range(columns // LANES))
    sigma = add_all(0, [part])[:1] * (1.0 / (ndev * rows * columns))

    lane16 = iota((16, LANES), 1) // CAP
    sub16 = iota((16, LANES), 0)
    own.wait()
    for g in range(chunks):
        lo = 1 if g == 0 else 0
        got = recv.at[pl.ds(g * chunk + lo, chunk - lo), pl.ds(0, MSG), :]
        pltpu.make_async_copy(got, got, a2a_recv.at[g]).wait()
        for h in range(chunk // 16):
            base = g * chunk + h * 16
            info = recv[pl.ds(base, 16), 32, :]
            off = jnp.sum(jnp.where(lane16 == sub16, info, 0.0), axis=0, keepdims=True).astype(i32)
            row_hot = (iota((rows, LANES), 0) == lax.shift_right_logical(off, 9)).astype(bf16)
            col = jnp.broadcast_to(lax.bitwise_and(off, 511).astype(f32), (LANES, LANES)).T.astype(i32)
            lane = iota((LANES, LANES), 1)
            shift = lax.bitwise_and(col, LANES - 1)
            index = lax.bitwise_and(lane - shift, LANES - 1)
            lag = lax.shift_right_logical(col, 7) + (lane < shift).astype(i32)
            spread = []
            for c in range(2):
                ab = []
                for half in range(2):
                    x = recv[pl.ds(base, 16), pl.ds((half * 2 + c) * CAP, CAP), :].reshape(LANES, LANES)
                    ab.append(jnp.take_along_axis(x, index, axis=1, mode="promise_in_bounds"))
                for t in range(4):
                    spread.append(
                        jnp.where(lag == t, ab[0], jnp.where(lag == t - 1, ab[1], 0.0))
                    )
            pieces = split3(jnp.concatenate(spread, axis=1))
            add = jnp.dot(
                jnp.concatenate([row_hot] * 3, axis=1), jnp.concatenate(pieces, axis=0), preferred_element_type=f32
            )
            if g == 0 and h == 0:
                deposit[...] = add
            elif g < chunks - 1 or h < chunk // 16 - 1:
                deposit[...] += add
            else:
                add = deposit[...] + add
                field[2, pl.ds(HALO, rows), pl.ds(0, columns)] = add[:, :columns]
                field[3, pl.ds(HALO, rows), pl.ds(0, columns)] = add[:, columns:]
    if chunks * (chunk // 16) == 1:
        field[2, pl.ds(HALO, rows), pl.ds(0, columns)] = deposit[:, :columns]
        field[3, pl.ds(HALO, rows), pl.ds(0, columns)] = deposit[:, columns:]

    offer(2)
    accept(2)

    def fold(x):
        return sum(x[:, k * LANES:(k + 1) * LANES] for k in range(columns // LANES))

    def apply(source, target, products):
        su, sv = source
        tu, tv = target

        def step(t, carry, mask, count_it):
            syy_old, sxy_old, acc = carry
            nxt = min(t + 1, tiles - 1) if isinstance(t, int) else t + 1
            here, there = tile_at(t), tile_at(nxt)
            u, v = su[here, :], sv[here, :]
            us, vs = south(u, su[there, :]), south(v, sv[there, :])
            s = nodes[here, :]
            exx = east(u) - u
            eyy = vs - v
            both = exx + eyy
            sxx = s * (exx + both)
            syy = s * (eyy + both)
            sxy = (0.5 * s) * ((us - u) + (east(v) - v))
            drag = field[1, here, :] - sigma
            au = (west(sxx) - sxx) + (north(sxy, sxy_old) - sxy) + drag * u
            av = (north(syy, syy_old) - syy) + (west(sxy) - sxy) + drag * v
            au = au * mask
            av = av * mask
            tu[here, :] = au
            tv[here, :] = av
            if count_it:
                acc = tuple(
                    a + fold(p[0] * q[0] + p[1] * q[1])
                    for a, (p, q) in zip(acc, [(((u, v), (au, av))[i], ((u, v), (au, av))[j]) for i, j in products])
                )
            return syy, sxy, acc

        zero = jnp.zeros((8, width), f32)
        carry = (zero, zero, tuple(jnp.zeros((8, LANES), f32) for _ in products))
        carry = step(0, carry, mask_main * above, False)
        carry = lax.fori_loop(1, tiles - 1, lambda t, c: step(t, c, mask_main, True), carry)
        carry = step(tiles - 1, carry, mask_main * below, False)
        return [jnp.sum(a, axis=0, keepdims=True) for a in carry[2]]

    f0 = (field.at[2], field.at[3])
    f1, f2, f3 = ((q.at[0], q.at[1]) for q in (q1, q2, q3))
    terms = apply(f0, f1, ((0, 0), (0, 1), (1, 1)))
    terms += apply(f1, f2, ((0, 1), (1, 1)))
    terms += apply(f2, f3, ((0, 1),))
    products = add_all(1, terms)

    m = [products[k:k + 1] / products[:1] for k in range(6)]

    def form(a, shifted):
        result = 0.0
        for i in range(len(a)):
            for j in range(i, len(a)):
                w = m[i + j + 1] + sigma * m[i + j] if shifted else m[i + j]
                term = a[i] * a[j] * w
                result = result + (term if i == j else 2.0 * term)
        return result

    one = jnp.ones((1, 1), f32)
    d, r, x, rr = [one], [one], [0.0 * one] * 3, one
    for k in range(3):
        alpha = rr / form(d, True)
        x = [x[i] + alpha * d[i] if i < len(d) else x[i] for i in range(3)]
        image = [sigma * d[i] for i in range(len(d))] + [0.0 * one]
        image = [image[i] + d[i - 1] if i else image[i] for i in range(len(image))]
        r = [(r[i] if i < len(r) else 0.0) - alpha * image[i] for i in range(len(image))]
        if k < 2:
            fresh = form(r, False)
            beta = fresh / rr
            d = [r[i] + (beta * d[i] if i < len(d) else 0.0) for i in range(len(r))]
            rr = fresh

    def finish(t, carry):
        here = pl.ds(pl.multiple_of(t * 8, 8), 8)
        padded = pl.ds(pl.multiple_of(t * 8 + HALO, 8), 8)
        main = pl.ds(0, columns)
        for c in range(2):
            a0, a1, a2, a3 = field[2 + c, padded, main], q1[c, padded, main], q2[c, padded, main], q3[c, padded, main]
            out_x[c, here, :] = x[0] * a0 + x[1] * a1 + x[2] * a2
            out_r[c, here, :] = r[0] * a0 + r[1] * a1 + r[2] * a2 + r[3] * a3
        return carry

    lax.fori_loop(0, rows // 8, finish, 0)

    for c in (0, 2):
        for copy in copies(c):
            copy.wait_send()
    for s in range(2):
        for copy in stage1(s) + stage2(s):
            copy.wait_send()
    for g in range(chunks):
        lo = 1 if g == 0 else 0
        sent = send.at[pl.ds(g * chunk + lo, chunk - lo), pl.ds(0, MSG), :]
        pltpu.make_async_copy(sent, sent, a2a_send.at[g]).wait()


def shards(n_gx, n_gy, misfit, owners, offsets, counts, viscosity, friction):
    ndev = n_gx * n_gy
    slots = owners.shape[0]
    rows, columns = viscosity.shape
    chunk = min(32, ndev)
    chunks = ndev // chunk
    near = min(8, n_gx)
    padded = (rows + 2 * HALO, columns + LANES)
    pixels = misfit.reshape(slots, 2, 2, LANES).transpose(0, 2, 1, 3).reshape(slots * 4, LANES)
    vmem = pl.BlockSpec(memory_space=pltpu.VMEM)
    smem = pl.BlockSpec(memory_space=pltpu.SMEM)
    out = jax.ShapeDtypeStruct((2, rows, columns), f32)
    dma = pltpu.SemaphoreType.DMA
    return pl.pallas_call(
        functools.partial(kernel, n_gx, n_gy, chunk),
        out_shape=(out, out),
        in_specs=[vmem, vmem, vmem, smem, vmem, vmem],
        out_specs=(vmem, vmem),
        scratch_shapes=[
            pltpu.VMEM((slots, 12 * LANES), bf16),
            pltpu.VMEM((ndev, PAD, LANES), f32),
            pltpu.VMEM((ndev, PAD, LANES), f32),
            pltpu.VMEM((rows, 2 * columns), f32),
            pltpu.VMEM((4,) + padded, f32),
            pltpu.VMEM(padded, f32),
            pltpu.VMEM((2,) + padded, f32),
            pltpu.VMEM((2,) + padded, f32),
            pltpu.VMEM((2,) + padded, f32),
            pltpu.VMEM((4, LANES, rows), f32),
            pltpu.VMEM((4, LANES, rows + 2 * LANES), f32),
            pltpu.VMEM((2, near + ndev // near, 8, LANES), f32),
            dma((chunks,)),
            dma((chunks,)),
            dma,
            dma((2, 8)),
            dma((2, 8)),
            dma((2, near + ndev // near)),
            dma((2, near + ndev // near)),
        ],
        compiler_params=pltpu.CompilerParams(
            collective_id=0, has_side_effects=True, vmem_limit_bytes=48 * 1024 * 1024
        ),
    )(
        pixels,
        owners.reshape(slots // LANES, LANES),
        offsets.reshape(slots // LANES, LANES),
        counts,
        viscosity,
        friction,
    )


def solution(mesh):
    in_specs = (
        P(("gx", "gy"), None, None),
        P(("gx", "gy")),
        P(("gx", "gy")),
        P(("gx", "gy")),
        P("gy", "gx"),
        P("gy", "gx"),
    )
    out_specs = (P(None, "gy", "gx"), P(None, "gy", "gx"))
    return jax.shard_map(
        functools.partial(shards, mesh.shape["gx"], mesh.shape["gy"]),
        mesh=mesh, in_specs=in_specs, out_specs=out_specs, check_vma=False,
    )
```

time: 702 us -> 103 us (0.15)
  blocking collectives: 330 us -> 0 us
  matrix products: 219 us -> 0 us
  Pallas kernels: 0 us -> 94.1 us
  starting transfers between devices: 58.8 us -> 0 us
  waiting for transfers between devices: 41 us -> 0 us
  other arithmetic: 26.8 us -> 0 us
  local copies, waits for them, and re-layouts: 15 us -> 6.98 us
    psum x5 -> x0, blocking collectives: 330 us -> none  [the longest x3 197 us: squares(): return lax.psum(jnp.sum(values * values), ('gx', 'gy'))]
    dot_general x34 -> x0, matrix products: 219 us -> none  [the longest x16 196 us: deposit(): placed = jnp.einsum('kcp,kpx->kcx', values, spread, precision=highest)]
    pallas_call x0 -> x1, Pallas kernels: none -> 94.1 us  [shards(): pl.pallas_call(functools.partial(kernel, n_gx, n_gy, chunk), out_shape=(o...]
    ppermute x16 -> x0, waiting for transfers between devices: 41 us -> none  [the longest x8 21.3 us: with_halo(): lax.ppermute(lax.slice_in_dim(block, block.shape[dim] - width, None, axis...]
    ppermute x16 -> x0, starting transfers between devices: 37.1 us -> none  [the longest x8 23.9 us: with_halo(): lax.ppermute(lax.slice_in_dim(block, block.shape[dim] - width, None, axis...]
    all_to_all x2 -> x0, starting transfers between devices: 21.7 us -> none  [the longest x1 11.5 us: shards(): lax.all_to_all(send_starts.reshape(ndev, capacity), ('gx', 'gy'), split_a...]
    reduce_sum x7 -> x0, other arithmetic: 8.19 us -> none  [the longest x3 4.78 us: squares(): return lax.psum(jnp.sum(values * values), ('gx', 'gy'))]
  transfers between devices with their start and end apart: 18 -> 0, of which waited for: 11 -> 0; matrix products, arithmetic and copies ran while one was open for 33% -> 0% of each run, Pallas kernels for 0% -> 0%
where the time goes in v1:
time: 103 us; the launch traced here: 102 us
  Pallas kernels  94.1 us (91%)
  local copies, waits for them, and re-layouts  6.98 us (7%)
  between operations  1.3 us (1%)
    pallas_call x1, Pallas kernels, shards(): pl.pallas_call(functools.partial(kernel, n_gx, n_gy, chunk), out_shape=(o...  94.1 us
    unnamed x12, local copies, waits for them, and re-layouts  6.98 us

profile of v1, /device:TPU:1, one launch (start us, length us, event | category | flops | bytes accessed | tf_op | source)
XLA Modules:
  0.0 102.4 jit_solution(2955697490956484457)
XLA Ops:
  1.3 0.0 copy-start
  1.3 1.6 %copy-done = f32[1024,2,256]{2,1,0:T(2,128)S(1)} copy-done((f32[1024,2,256]{2,1,0:T(2,128)S(1)}, f32[1024,2,256]{2,1,0:T(2,128)}, u32[]{:S(2)}) %copy-start) | copy-done | bytes 2097176
  2.9 0.0 copy-start.1
  2.9 1.0 %copy-done.1 = f32[256,512]{1,0:T(8,128)S(1)} copy-done((f32[256,512]{1,0:T(8,128)S(1)}, f32[256,512]{1,0:T(8,128)}, u32[]{:S(2)}) %copy-start.1) | copy-done | bytes 524312
  3.9 0.0 copy-start.2
  3.9 1.0 %copy-done.2 = f32[256,512]{1,0:T(8,128)S(1)} copy-done((f32[256,512]{1,0:T(8,128)S(1)}, f32[256,512]{1,0:T(8,128)}, u32[]{:S(2)}) %copy-start.2) | copy-done | bytes 524312
  5.0 0.0 copy-start.3
  5.0 0.7 copy-done.3
  5.6 0.0 copy-start.4
  5.6 0.7 copy-done.4
  6.3 94.1 %shard_map.77 = (f32[2,256,512]{2,1,0:T(8,128)S(1)}, f32[2,256,512]{2,1,0:T(8,128)S(1)}) custom-call(f32[4096,128]{1,0:T(8,128)S(1)} %bitcast.7, s32[8,128]{1,0:T(8,128)S(1)} %bitcast.8, s32[8,128]{1,0:T(8,128)S(1)} %bitcast.9, s32[1]{0:T(128)S(6)} %copy.11.counts, f32[256,512]{1,0:T(8,128)S(1)} %copy-done.1, f32[256,512]{1,0:T(8,128)S(1)} %copy-done.2), custom_call_target="tpu_custom_call" | custom-call | tf_op jit(solution)/shard_map/pallas_call | solution.py:416
  100.4 1.0 copy.12
  101.4 1.0 copy.13
Async XLA Ops:
  1.3 1.6 %copy-start = (f32[1024,2,256]{2,1,0:T(2,128)S(1)}, f32[1024,2,256]{2,1,0:T(2,128)}, u32[]{:S(2)}) copy-start(f32[1024,2,256]{2,1,0:T(2,128)} %param.6) | copy-start | bytes 6291460
  2.9 1.0 %copy-start.1 = (f32[256,512]{1,0:T(8,128)S(1)}, f32[256,512]{1,0:T(8,128)}, u32[]{:S(2)}) copy-start(f32[256,512]{1,0:T(8,128)} %viscosity.1) | copy-start | bytes 1572868
  3.9 1.0 %copy-start.2 = (f32[256,512]{1,0:T(8,128)S(1)}, f32[256,512]{1,0:T(8,128)}, u32[]{:S(2)}) copy-start(f32[256,512]{1,0:T(8,128)} %friction.1) | copy-start | bytes 1572868
  5.0 0.7 copy-start.3
  5.6 0.7 copy-start.4

commit v2 on v1

--- a/solution.py
+++ b/solution.py
@@ -13,6 +13,8 @@
 HALO = 8
 MSG = 33
 PAD = 40
+STRIDE, BACK = 37, 45
+GRAIN = 1024.0
 bf16, f32, i32 = jnp.bfloat16, jnp.float32, jnp.int32
 
 
@@ -36,26 +38,46 @@
 
 def kernel(
     n_gx, n_gy, chunk,
-    misfit, owners, offsets, counts, viscosity, friction, out_x, out_r,
-    parts, send, recv, deposit, field, nodes, q1, q2, q3, strips, halo, sums,
-    a2a_send, a2a_recv, self_sem, ex_send, ex_recv, ar_send, ar_recv,
+    misfit_hbm, owners_hbm, offsets_hbm, counts, viscosity_hbm, friction_hbm, out_x, out_r,
+    misfit, owners, offsets, parts, send, recv, deposit, field, nodes, q1, q2, q3, strips, halo, sums,
+    in_sem, a2a_send, a2a_recv, self_sem, ex_send, ex_recv, ar_send, ar_recv,
 ):
     ndev = n_gx * n_gy
     ix, iy = lax.axis_index("gx"), lax.axis_index("gy")
     me = ix * n_gy + iy
     slots = misfit.shape[0] // 4
-    rows, columns = viscosity.shape
+    rows, columns = viscosity_hbm.shape
     chunks = ndev // chunk
     keys = chunk * CAP
+    gx_dims = (4, 4, 2) if n_gx == 32 else (n_gx // 2, 2)
+
+    def ahead(p):
+        dev = lax.rem(me + p * STRIDE, ndev)
+        return dev // n_gy, lax.rem(dev, n_gy)
 
     barrier = pltpu.get_barrier_semaphore()
 
     def greet(p, carry):
-        dev = lax.rem(me + p, ndev)
-        pl.semaphore_signal(barrier, inc=1, device_id=(dev // n_gy, lax.rem(dev, n_gy)), device_id_type=MESH)
+        pl.semaphore_signal(barrier, inc=1, device_id=ahead(p), device_id_type=MESH)
         return carry
 
+    loads = [
+        pltpu.make_async_copy(src, dst, in_sem.at[k])
+        for k, (src, dst) in enumerate(
+            (
+                (owners_hbm, owners),
+                (offsets_hbm, offsets),
+                (viscosity_hbm, field.at[0, pl.ds(HALO, rows), pl.ds(0, columns)]),
+                (friction_hbm, field.at[1, pl.ds(HALO, rows), pl.ds(0, columns)]),
+                (misfit_hbm, misfit),
+            )
+        )
+    ]
+    for load in loads:
+        load.start()
     lax.fori_loop(1, ndev, greet, 0)
+    loads[0].wait()
+    loads[1].wait()
 
     count = counts[0]
     lane_blocks = slots // LANES
@@ -66,7 +88,7 @@
         own = owners[pl.ds(b, 1), :]
         off = offsets[pl.ds(b, 1), :]
         live = (iota((1, LANES), 1) + b * LANES) < count
-        rel = jnp.where(live, lax.rem(own - me + ndev, ndev), -1)
+        rel = jnp.where(live, lax.rem((own - me + ndev) * BACK, ndev), -1)
         hot = (iota((ndev, LANES), 0) == rel).astype(f32)
         before = jnp.dot(hot.astype(bf16), upper, preferred_element_type=f32) + carry
         rank = jnp.sum(hot * before, axis=0, keepdims=True).astype(i32)
@@ -82,17 +104,27 @@
     weight = jnp.concatenate(weights, axis=1)
     meta = lax.dot_general(hot, weight, (((1,), (1,)), ((), ())), preferred_element_type=f32)
     meta = meta[:, :LANES] * 512.0 + meta[:, LANES:]
-    send[:, 32, :] = meta
-
+
+    loads[2].wait()
+    loads[3].wait()
+
+    def share_tile(t, total):
+        here = pl.ds(pl.multiple_of(t * 8 + HALO, 8), 8)
+        return total + 10.0 * field[0, here, pl.ds(0, columns)] + field[1, here, pl.ds(0, columns)]
+
+    share = lax.fori_loop(0, rows // 8, share_tile, jnp.zeros((8, columns), f32), unroll=4)
+    share = jnp.sum(jnp.sum(share, axis=0, keepdims=True), axis=1, keepdims=True)
+    share = jnp.round(share * (GRAIN / (rows * columns)))
+    send[:, 32, :] = jnp.where(iota((ndev, LANES), 1) < 64, meta, share)
+
+    loads[4].wait()
     for t in range(4):
         hi, mid, low = split3(misfit[pl.ds(t, slots, stride=4), :])
         parts[:, pl.ds(t * LANES, LANES)] = hi
         parts[:, pl.ds((4 + t) * LANES, LANES)] = mid
         parts[:, pl.ds((8 + t) * LANES, LANES)] = low
 
-    pl.semaphore_wait(barrier, ndev - 1)
-
-    def pack(g, carry):
+    def pack(g):
         place = ((iota((keys, slots), 0) + g * keys) == target).astype(bf16)
         packed = jnp.dot(place, parts[...], preferred_element_type=f32)
         packed = packed[:, :512] + packed[:, 512:1024] + packed[:, 1024:]
@@ -101,21 +133,14 @@
                 chunk, CAP, LANES
             )
 
-        def push(i, carry):
-            p = g * chunk + i
-            dev = lax.rem(me + p, ndev)
+    def push(g):
+        def one(p, carry):
             remote(
-                send.at[p, pl.ds(0, MSG), :], recv.at[p, pl.ds(0, MSG), :], a2a_send.at[g], a2a_recv.at[g],
-                (dev // n_gy, lax.rem(dev, n_gy)),
+                send.at[p, pl.ds(0, MSG), :], recv.at[p, pl.ds(0, MSG), :], a2a_send.at[g], a2a_recv.at[g], ahead(p)
             ).start()
             return carry
 
-        lax.fori_loop(jnp.where(g == 0, 1, 0), chunk, push, 0)
-        return carry
-
-    lax.fori_loop(0, chunks, pack, 0)
-    own = pltpu.make_async_copy(send.at[0, pl.ds(0, MSG), :], recv.at[0, pl.ds(0, MSG), :], self_sem)
-    own.start()
+        lax.fori_loop(max(g * chunk, 1), (g + 1) * chunk, one, 0)
 
     left, right = lax.rem(ix + n_gx - 1, n_gx), lax.rem(ix + 1, n_gx)
     up, down = lax.rem(iy + n_gy - 1, n_gy), lax.rem(iy + 1, n_gy)
@@ -153,8 +178,6 @@
                     iota((LANES, LANES), 1) < 64, field[f, at, pl.ds(0, LANES)], field[f, at, pl.ds(columns - LANES, LANES)]
                 )
                 strips[f, :, pl.ds(j * LANES, LANES)] = mix.T
-        for copy in copies(c):
-            copy.start()
 
     def accept(c):
         for copy in copies(c):
@@ -172,53 +195,52 @@
 
     for f in range(4):
         halo[f, pl.ds(8, LANES - 16), :] = jnp.zeros((LANES - 16, halo.shape[2]), f32)
-    field[0, pl.ds(HALO, rows), pl.ds(0, columns)] = viscosity[...]
-    field[1, pl.ds(HALO, rows), pl.ds(0, columns)] = friction[...]
     offer(0)
-
-    near = min(8, n_gx)
-    far = ndev // near
-
-    def stage1(s):
-        low, high = lax.rem(ix, near), ix // near * near
-        return [
-            remote(sums.at[s, 0], sums.at[s, k], ar_send.at[s, k], ar_recv.at[s, k], (high + lax.rem(low + k, near), iy))
-            for k in range(1, near)
-        ]
-
-    def stage2(s):
-        low = lax.rem(ix, near)
-        group = ix // near * n_gy + iy
+    pack(0)
+    pl.semaphore_wait(barrier, ndev - 1)
+    for copy in copies(0):
+        copy.start()
+    push(0)
+    own = pltpu.make_async_copy(send.at[0, pl.ds(0, MSG), :], recv.at[0, pl.ds(0, MSG), :], self_sem)
+    own.start()
+    for g in range(1, chunks):
+        pack(g)
+        push(g)
+
+    shifts = []
+    for k in range(1, ndev):
+        rest, shift, far = k, [], 0
+        for size in (n_gy,) + gx_dims[::-1]:
+            shift.append(rest % size)
+            far += min(rest % size, size - rest % size)
+            rest //= size
+        shifts.append((-far, k, shift[0], shift[:0:-1]))
+    shifts.sort()
+
+    def sum_copies():
         result = []
-        for k in range(1, far):
-            other = lax.rem(group + k, far)
+        for _, k, dy, dx in shifts:
+            to, unit = 0, n_gx
+            for size, d in zip(gx_dims, dx):
+                unit //= size
+                to = to + lax.rem(lax.rem(ix // unit, size) + d, size) * unit
             result.append(
                 remote(
-                    sums.at[s, near], sums.at[s, near + k], ar_send.at[s, near + k], ar_recv.at[s, near + k],
-                    (other // n_gy * near + low, lax.rem(other, n_gy)),
+                    sums.at[pl.ds(0, 1), :], sums.at[pl.ds(k, 1), :], ar_send, ar_recv, (to, lax.rem(iy + dy, n_gy))
                 )
             )
         return result
 
-    def add_all(s, terms):
+    def add_all(terms):
         terms = list(terms) + [jnp.zeros((1, LANES), f32)] * (8 - len(terms))
-        sums[s, 0] = jnp.concatenate(terms, axis=0)
-        for copy in stage1(s):
+        totals = jnp.sum(jnp.concatenate(terms, axis=0), axis=1, keepdims=True)
+        totals = jnp.where(iota((8, LANES), 0) == iota((8, LANES), 1), totals, 0.0)
+        sums[pl.ds(0, 1), :] = jnp.sum(totals, axis=0, keepdims=True)
+        for copy in sum_copies():
             copy.start()
-        for copy in stage1(s):
-            copy.wait_recv()
-        total = sums[s, 0]
-        for k in range(1, near):
-            total = total + sums[s, k]
-        sums[s, near] = total
-        for copy in stage2(s):
-            copy.start()
-        for copy in stage2(s):
-            copy.wait_recv()
-        total = sums[s, near]
-        for k in range(1, far):
-            total = total + sums[s, near + k]
-        return jnp.sum(total, axis=1, keepdims=True)
+        others = sums.at[pl.ds(1, ndev - 1), :]
+        pltpu.make_async_copy(others, others, ar_recv).wait()
+        return jnp.sum(sums[...], axis=0, keepdims=True)
 
     tiles = (rows + 2 * HALO) // 8
     width = columns + LANES
@@ -244,22 +266,19 @@
 
     accept(0)
 
-    def node_tile(t, total):
+    def node_tile(t, carry):
         here = field[0, tile_at(t), :]
         following = field[0, tile_at(jnp.minimum(t + 1, tiles - 1)), :]
         pair = here + south(here, following)
-        doubled = 0.5 * (pair + east(pair))
-        nodes[tile_at(t), :] = doubled
-        return total + 5.0 * doubled + field[1, tile_at(t), :]
-
-    total = lax.fori_loop(0, tiles, node_tile, jnp.zeros((8, width), f32))
-    total = jnp.sum(total, axis=0, keepdims=True)
-    part = sum(total[:, k * LANES:(k + 1) * LANES] for k in range(columns // LANES))
-    sigma = add_all(0, [part])[:1] * (1.0 / (ndev * rows * columns))
+        nodes[tile_at(t), :] = 0.5 * (pair + east(pair))
+        return carry
+
+    lax.fori_loop(0, tiles, node_tile, 0, unroll=2)
 
     lane16 = iota((16, LANES), 1) // CAP
     sub16 = iota((16, LANES), 0)
     own.wait()
+    shift_sum = jnp.zeros((16, LANES), f32)
     for g in range(chunks):
         lo = 1 if g == 0 else 0
         got = recv.at[pl.ds(g * chunk + lo, chunk - lo), pl.ds(0, MSG), :]
@@ -267,6 +286,8 @@
         for h in range(chunk // 16):
             base = g * chunk + h * 16
             info = recv[pl.ds(base, 16), 32, :]
+            shift_sum = shift_sum + info
+            info = jnp.where(sub16 < 8, info, pltpu.roll(info, 64, 1))
             off = jnp.sum(jnp.where(lane16 == sub16, info, 0.0), axis=0, keepdims=True).astype(i32)
             row_hot = (iota((rows, LANES), 0) == lax.shift_right_logical(off, 9)).astype(bf16)
             col = jnp.broadcast_to(lax.bitwise_and(off, 511).astype(f32), (LANES, LANES)).T.astype(i32)
@@ -300,7 +321,10 @@
         field[2, pl.ds(HALO, rows), pl.ds(0, columns)] = deposit[:, :columns]
         field[3, pl.ds(HALO, rows), pl.ds(0, columns)] = deposit[:, columns:]
 
+    sigma = jnp.sum(shift_sum, axis=0, keepdims=True)[:, 64:65] * (1.0 / (ndev * GRAIN))
     offer(2)
+    for copy in copies(2):
+        copy.start()
     accept(2)
 
     def fold(x):
@@ -340,7 +364,7 @@
         zero = jnp.zeros((8, width), f32)
         carry = (zero, zero, tuple(jnp.zeros((8, LANES), f32) for _ in products))
         carry = step(0, carry, mask_main * above, False)
-        carry = lax.fori_loop(1, tiles - 1, lambda t, c: step(t, c, mask_main, True), carry)
+        carry = lax.fori_loop(1, tiles - 1, lambda t, c: step(t, c, mask_main, True), carry, unroll=8)
         carry = step(tiles - 1, carry, mask_main * below, False)
         return [jnp.sum(a, axis=0, keepdims=True) for a in carry[2]]
 
@@ -349,9 +373,9 @@
     terms = apply(f0, f1, ((0, 0), (0, 1), (1, 1)))
     terms += apply(f1, f2, ((0, 1), (1, 1)))
     terms += apply(f2, f3, ((0, 1),))
-    products = add_all(1, terms)
-
-    m = [products[k:k + 1] / products[:1] for k in range(6)]
+    products = add_all(terms)
+
+    m = [products[:, k:k + 1] / products[:, :1] for k in range(6)]
 
     def form(a, shifted):
         result = 0.0
@@ -386,14 +410,13 @@
             out_r[c, here, :] = r[0] * a0 + r[1] * a1 + r[2] * a2 + r[3] * a3
         return carry
 
-    lax.fori_loop(0, rows // 8, finish, 0)
+    lax.fori_loop(0, rows // 8, finish, 0, unroll=4)
 
     for c in (0, 2):
         for copy in copies(c):
             copy.wait_send()
-    for s in range(2):
-        for copy in stage1(s) + stage2(s):
-            copy.wait_send()
+    others = sums.at[pl.ds(1, ndev - 1), :]
+    pltpu.make_async_copy(others, others, ar_send).wait()
     for g in range(chunks):
         lo = 1 if g == 0 else 0
         sent = send.at[pl.ds(g * chunk + lo, chunk - lo), pl.ds(0, MSG), :]
@@ -406,19 +429,22 @@
     rows, columns = viscosity.shape
     chunk = min(32, ndev)
     chunks = ndev // chunk
-    near = min(8, n_gx)
     padded = (rows + 2 * HALO, columns + LANES)
     pixels = misfit.reshape(slots, 2, 2, LANES).transpose(0, 2, 1, 3).reshape(slots * 4, LANES)
     vmem = pl.BlockSpec(memory_space=pltpu.VMEM)
+    hbm = pl.BlockSpec(memory_space=pltpu.HBM)
     smem = pl.BlockSpec(memory_space=pltpu.SMEM)
     out = jax.ShapeDtypeStruct((2, rows, columns), f32)
     dma = pltpu.SemaphoreType.DMA
     return pl.pallas_call(
         functools.partial(kernel, n_gx, n_gy, chunk),
         out_shape=(out, out),
-        in_specs=[vmem, vmem, vmem, smem, vmem, vmem],
+        in_specs=[hbm, hbm, hbm, smem, hbm, hbm],
         out_specs=(vmem, vmem),
         scratch_shapes=[
+            pltpu.VMEM((slots * 4, LANES), f32),
+            pltpu.VMEM((slots // LANES, LANES), i32),
+            pltpu.VMEM((slots // LANES, LANES), i32),
             pltpu.VMEM((slots, 12 * LANES), bf16),
             pltpu.VMEM((ndev, PAD, LANES), f32),
             pltpu.VMEM((ndev, PAD, LANES), f32),
@@ -430,17 +456,18 @@
             pltpu.VMEM((2,) + padded, f32),
             pltpu.VMEM((4, LANES, rows), f32),
             pltpu.VMEM((4, LANES, rows + 2 * LANES), f32),
-            pltpu.VMEM((2, near + ndev // near, 8, LANES), f32),
+            pltpu.VMEM((ndev, LANES), f32),
+            dma((5,)),
             dma((chunks,)),
             dma((chunks,)),
             dma,
             dma((2, 8)),
             dma((2, 8)),
-            dma((2, near + ndev // near)),
-            dma((2, near + ndev // near)),
+            dma,
+            dma,
         ],
         compiler_params=pltpu.CompilerParams(
-            collective_id=0, has_side_effects=True, vmem_limit_bytes=48 * 1024 * 1024
+            collective_id=0, has_side_effects=True, vmem_limit_bytes=54 * 1024 * 1024
         ),
     )(
         pixels,

time: 103 us -> 65 us (0.63)
  Pallas kernels: 94.1 us -> 60.2 us
  local copies, waits for them, and re-layouts: 6.98 us -> 3.32 us
    pallas_call x1, Pallas kernels: 94.1 us -> 60.2 us  [shards(): pl.pallas_call(functools.partial(kernel, n_gx, n_gy, chunk), out_shape=(o...]
    unnamed x12 -> x4, local copies, waits for them, and re-layouts: 6.98 us -> 3.32 us
where the time goes in v2:
time: 65 us; the launch traced here: 64.8 us
  Pallas kernels  60.2 us (93%)
  local copies, waits for them, and re-layouts  3.32 us (5%)
  between operations  1.29 us (2%)
    pallas_call x1, Pallas kernels, shards(): pl.pallas_call(functools.partial(kernel, n_gx, n_gy, chunk), out_shape=(o...  60.2 us
    unnamed x4, local copies, waits for them, and re-layouts  3.32 us

profile of v2, /device:TPU:1, one launch (start us, length us, event | category | flops | bytes accessed | tf_op | source)
XLA Modules:
  0.0 64.8 jit_solution(10669460714913651158)
XLA Ops:
  1.3 60.2 %shard_map.77 = (f32[2,256,512]{2,1,0:T(8,128)}, f32[2,256,512]{2,1,0:T(8,128)}) custom-call(f32[4096,128]{1,0:T(8,128)} %bitcast.7, s32[8,128]{1,0:T(8,128)} %bitcast.8, s32[8,128]{1,0:T(8,128)} %bitcast.9, s32[1]{0:T(128)S(6)} %copy.11.counts, f32[256,512]{1,0:T(8,128)} %viscosity_hbm.1, f32[256,512]{1,0:T(8,128)} %friction_hbm.1), custom_call_target="tpu_custom_call" | custom-call | tf_op jit(solution)/shard_map/pallas_call | solution.py:439
  61.5 0.0 copy-start
  61.5 2.4 %copy.12 = f32[2,256,512]{2,1,0:T(8,128)} copy(f32[2,256,512]{2,1,0:T(8,128)} %get-tuple-element.4) | data formatting | bytes 2097152
  63.8 0.0 copy-done
  63.8 1.0 %copy.13 = f32[2,256,512]{2,1,0:T(8,128)} copy(f32[2,256,512]{2,1,0:T(8,128)S(1)} %copy-done) | data formatting | bytes 2097152
Async XLA Ops:
  61.5 2.4 %copy-start = (f32[2,256,512]{2,1,0:T(8,128)S(1)}, f32[2,256,512]{2,1,0:T(8,128)}, u32[]{:S(2)}) copy-start(f32[2,256,512]{2,1,0:T(8,128)} %get-tuple-element.5) | copy-start | bytes 3145732

commit v3 on v2

--- a/solution.py
+++ b/solution.py
@@ -2,6 +2,7 @@
 
 import jax
 import jax.numpy as jnp
+import numpy as np
 from jax import lax
 from jax.experimental import pallas as pl
 from jax.experimental.pallas import tpu as pltpu
@@ -13,7 +14,6 @@
 HALO = 8
 MSG = 33
 PAD = 40
-STRIDE, BACK = 37, 45
 GRAIN = 1024.0
 bf16, f32, i32 = jnp.bfloat16, jnp.float32, jnp.int32
 
@@ -36,11 +36,37 @@
     )
 
 
+def plan(n_gx, n_gy):
+    sizes = ((4, 4, 2) if n_gx == 32 else (n_gx // 2, 2)) + (n_gy,)
+    ndev = n_gx * n_gy
+    shifts = []
+    for p in range(1, ndev):
+        rest, shift = p * 37 % ndev, []
+        for size in sizes[::-1]:
+            shift.insert(0, rest % size)
+            rest //= size
+        shifts.append(tuple(shift))
+
+    def hops(shift):
+        return sum(min(d, n - d) for d, n in zip(shift[:-2] + shift[-1:], sizes[:-2] + sizes[-1:]))
+
+    near = sorted(shifts, key=lambda s: -hops(s))[-30 * ndev // 128:]
+    order = [(0,) * len(sizes)] + [s for s in shifts if s not in near] + near
+    return sizes, order, sorted(shifts, key=lambda s: -hops(s))
+
+
+def code(shift, sizes):
+    result = 0
+    for d, n in zip(shift, sizes):
+        result = result * n + d
+    return result
+
+
 def kernel(
     n_gx, n_gy, chunk,
-    misfit_hbm, owners_hbm, offsets_hbm, counts, viscosity_hbm, friction_hbm, out_x, out_r,
-    misfit, owners, offsets, parts, send, recv, deposit, field, nodes, q1, q2, q3, strips, halo, sums,
-    in_sem, a2a_send, a2a_recv, self_sem, ex_send, ex_recv, ar_send, ar_recv,
+    misfit_hbm, owners_hbm, offsets_hbm, counts, viscosity_hbm, friction_hbm, codes_hbm, basis, weights_out,
+    misfit, owners, offsets, codes, parts, send, recv, deposit, field, nodes, q1, q2, q3, strips, halo, sums,
+    in_sem, out_sem, a2a_send, a2a_recv, self_sem, ex_send, ex_recv, ar_send, ar_recv,
 ):
     ndev = n_gx * n_gy
     ix, iy = lax.axis_index("gx"), lax.axis_index("gy")
@@ -49,17 +75,20 @@
     rows, columns = viscosity_hbm.shape
     chunks = ndev // chunk
     keys = chunk * CAP
-    gx_dims = (4, 4, 2) if n_gx == 32 else (n_gx // 2, 2)
-
-    def ahead(p):
-        dev = lax.rem(me + p * STRIDE, ndev)
-        return dev // n_gy, lax.rem(dev, n_gy)
-
-    barrier = pltpu.get_barrier_semaphore()
-
-    def greet(p, carry):
-        pl.semaphore_signal(barrier, inc=1, device_id=ahead(p), device_id_type=MESH)
-        return carry
+    sizes, order, farthest = plan(n_gx, n_gy)
+
+    def split(x, y):
+        result, unit = [], n_gx
+        for n in sizes[:-1]:
+            unit //= n
+            result.append(lax.rem(x // unit, n))
+        return result + [y]
+
+    here = split(ix, iy)
+
+    def peer(shift):
+        at = [lax.rem(a + d, n) for a, d, n in zip(here, shift, sizes)]
+        return code(at[:-1], sizes[:-1]), at[-1]
 
     loads = [
         pltpu.make_async_copy(src, dst, in_sem.at[k])
@@ -67,6 +96,7 @@
             (
                 (owners_hbm, owners),
                 (offsets_hbm, offsets),
+                (codes_hbm, codes),
                 (viscosity_hbm, field.at[0, pl.ds(HALO, rows), pl.ds(0, columns)]),
                 (friction_hbm, field.at[1, pl.ds(HALO, rows), pl.ds(0, columns)]),
                 (misfit_hbm, misfit),
@@ -75,9 +105,12 @@
     ]
     for load in loads:
         load.start()
-    lax.fori_loop(1, ndev, greet, 0)
-    loads[0].wait()
-    loads[1].wait()
+    barrier = pltpu.get_barrier_semaphore()
+    for shift in farthest:
+        pl.semaphore_signal(barrier, inc=1, device_id=peer(shift), device_id_type=MESH)
+
+    for load in loads[:3]:
+        load.wait()
 
     count = counts[0]
     lane_blocks = slots // LANES
@@ -88,12 +121,14 @@
         own = owners[pl.ds(b, 1), :]
         off = offsets[pl.ds(b, 1), :]
         live = (iota((1, LANES), 1) + b * LANES) < count
-        rel = jnp.where(live, lax.rem((own - me + ndev) * BACK, ndev), -1)
-        hot = (iota((ndev, LANES), 0) == rel).astype(f32)
+        theirs = split(own // n_gy, lax.rem(own, n_gy))
+        rel = code([lax.rem(a - b + n, n) for a, b, n in zip(theirs, here, sizes)], sizes)
+        hot = (codes[:, :LANES] == jnp.where(live, rel, -1)).astype(f32)
+        number = jnp.sum(hot * iota((ndev, LANES), 0).astype(f32), axis=0, keepdims=True).astype(i32)
         before = jnp.dot(hot.astype(bf16), upper, preferred_element_type=f32) + carry
         rank = jnp.sum(hot * before, axis=0, keepdims=True).astype(i32)
         carry = carry + jnp.sum(hot, axis=1, keepdims=True)
-        targets.append(jnp.where(live, rel * CAP + rank, -1))
+        targets.append(jnp.where(live, number * CAP + rank, -1))
         hots.append(hot.astype(bf16))
         mine = lax.rem(iota((LANES, LANES), 0), CAP) == rank
         row_part = jnp.where(mine, lax.shift_right_logical(off, 9).astype(f32), 0.0)
@@ -105,19 +140,19 @@
     meta = lax.dot_general(hot, weight, (((1,), (1,)), ((), ())), preferred_element_type=f32)
     meta = meta[:, :LANES] * 512.0 + meta[:, LANES:]
 
-    loads[2].wait()
     loads[3].wait()
+    loads[4].wait()
 
     def share_tile(t, total):
-        here = pl.ds(pl.multiple_of(t * 8 + HALO, 8), 8)
-        return total + 10.0 * field[0, here, pl.ds(0, columns)] + field[1, here, pl.ds(0, columns)]
+        at = pl.ds(pl.multiple_of(t * 8 + HALO, 8), 8)
+        return total + 10.0 * field[0, at, pl.ds(0, columns)] + field[1, at, pl.ds(0, columns)]
 
     share = lax.fori_loop(0, rows // 8, share_tile, jnp.zeros((8, columns), f32), unroll=4)
     share = jnp.sum(jnp.sum(share, axis=0, keepdims=True), axis=1, keepdims=True)
     share = jnp.round(share * (GRAIN / (rows * columns)))
     send[:, 32, :] = jnp.where(iota((ndev, LANES), 1) < 64, meta, share)
 
-    loads[4].wait()
+    loads[5].wait()
     for t in range(4):
         hi, mid, low = split3(misfit[pl.ds(t, slots, stride=4), :])
         parts[:, pl.ds(t * LANES, LANES)] = hi
@@ -134,13 +169,10 @@
             )
 
     def push(g):
-        def one(p, carry):
+        for p in range(max(g * chunk, 1), (g + 1) * chunk):
             remote(
-                send.at[p, pl.ds(0, MSG), :], recv.at[p, pl.ds(0, MSG), :], a2a_send.at[g], a2a_recv.at[g], ahead(p)
+                send.at[p, pl.ds(0, MSG), :], recv.at[p, pl.ds(0, MSG), :], a2a_send.at[g], a2a_recv.at[g], peer(order[p])
             ).start()
-            return carry
-
-        lax.fori_loop(max(g * chunk, 1), (g + 1) * chunk, one, 0)
 
     left, right = lax.rem(ix + n_gx - 1, n_gx), lax.rem(ix + 1, n_gx)
     up, down = lax.rem(iy + n_gy - 1, n_gy), lax.rem(iy + 1, n_gy)
@@ -195,41 +227,23 @@
 
     for f in range(4):
         halo[f, pl.ds(8, LANES - 16), :] = jnp.zeros((LANES - 16, halo.shape[2]), f32)
-    offer(0)
     pack(0)
     pl.semaphore_wait(barrier, ndev - 1)
+    push(0)
+    offer(0)
     for copy in copies(0):
         copy.start()
-    push(0)
     own = pltpu.make_async_copy(send.at[0, pl.ds(0, MSG), :], recv.at[0, pl.ds(0, MSG), :], self_sem)
     own.start()
     for g in range(1, chunks):
         pack(g)
         push(g)
 
-    shifts = []
-    for k in range(1, ndev):
-        rest, shift, far = k, [], 0
-        for size in (n_gy,) + gx_dims[::-1]:
-            shift.append(rest % size)
-            far += min(rest % size, size - rest % size)
-            rest //= size
-        shifts.append((-far, k, shift[0], shift[:0:-1]))
-    shifts.sort()
-
     def sum_copies():
-        result = []
-        for _, k, dy, dx in shifts:
-            to, unit = 0, n_gx
-            for size, d in zip(gx_dims, dx):
-                unit //= size
-                to = to + lax.rem(lax.rem(ix // unit, size) + d, size) * unit
-            result.append(
-                remote(
-                    sums.at[pl.ds(0, 1), :], sums.at[pl.ds(k, 1), :], ar_send, ar_recv, (to, lax.rem(iy + dy, n_gy))
-                )
-            )
-        return result
+        return [
+            remote(sums.at[pl.ds(0, 1), :], sums.at[pl.ds(k, 1), :], ar_send, ar_recv, peer(shift))
+            for k, shift in enumerate(farthest, 1)
+        ]
 
     def add_all(terms):
         terms = list(terms) + [jnp.zeros((1, LANES), f32)] * (8 - len(terms))
@@ -373,6 +387,12 @@
     terms = apply(f0, f1, ((0, 0), (0, 1), (1, 1)))
     terms += apply(f1, f2, ((0, 1), (1, 1)))
     terms += apply(f2, f3, ((0, 1),))
+    saves = [
+        pltpu.make_async_copy(src.at[pl.ds(at, 2), pl.ds(HALO, rows), pl.ds(0, columns)], basis.at[k], out_sem.at[k])
+        for k, (src, at) in enumerate(((field, 2), (q1, 0), (q2, 0), (q3, 0)))
+    ]
+    for save in saves:
+        save.start()
     products = add_all(terms)
 
     m = [products[:, k:k + 1] / products[:, :1] for k in range(6)]
@@ -400,17 +420,9 @@
             d = [r[i] + (beta * d[i] if i < len(d) else 0.0) for i in range(len(r))]
             rr = fresh
 
-    def finish(t, carry):
-        here = pl.ds(pl.multiple_of(t * 8, 8), 8)
-        padded = pl.ds(pl.multiple_of(t * 8 + HALO, 8), 8)
-        main = pl.ds(0, columns)
-        for c in range(2):
-            a0, a1, a2, a3 = field[2 + c, padded, main], q1[c, padded, main], q2[c, padded, main], q3[c, padded, main]
-            out_x[c, here, :] = x[0] * a0 + x[1] * a1 + x[2] * a2
-            out_r[c, here, :] = r[0] * a0 + r[1] * a1 + r[2] * a2 + r[3] * a3
-        return carry
-
-    lax.fori_loop(0, rows // 8, finish, 0, unroll=4)
+    weights_out[...] = jnp.concatenate([jnp.broadcast_to(w, (1, LANES)) for w in x + r + [one]], axis=0)
+    for save in saves:
+        save.wait()
 
     for c in (0, 2):
         for copy in copies(c):
@@ -421,6 +433,14 @@
         lo = 1 if g == 0 else 0
         sent = send.at[pl.ds(g * chunk + lo, chunk - lo), pl.ds(0, MSG), :]
         pltpu.make_async_copy(sent, sent, a2a_send.at[g]).wait()
+
+
+def combine(weights, basis, out_x, out_r):
+    w = [weights[k:k + 1, :1] for k in range(7)]
+    for c in range(2):
+        a0, a1, a2, a3 = (basis[k, c] for k in range(4))
+        out_x[c] = w[0] * a0 + w[1] * a1 + w[2] * a2
+        out_r[c] = w[3] * a0 + w[4] * a1 + w[5] * a2 + w[6] * a3
 
 
 def shards(n_gx, n_gy, misfit, owners, offsets, counts, viscosity, friction):
@@ -435,16 +455,19 @@
     hbm = pl.BlockSpec(memory_space=pltpu.HBM)
     smem = pl.BlockSpec(memory_space=pltpu.SMEM)
     out = jax.ShapeDtypeStruct((2, rows, columns), f32)
+    sizes, order, _ = plan(n_gx, n_gy)
+    codes = np.tile(np.array([[code(s, sizes)] for s in order], np.int32), (1, LANES))
     dma = pltpu.SemaphoreType.DMA
-    return pl.pallas_call(
+    basis, weights = pl.pallas_call(
         functools.partial(kernel, n_gx, n_gy, chunk),
-        out_shape=(out, out),
-        in_specs=[hbm, hbm, hbm, smem, hbm, hbm],
-        out_specs=(vmem, vmem),
+        out_shape=(jax.ShapeDtypeStruct((4, 2, rows, columns), f32), jax.ShapeDtypeStruct((8, LANES), f32)),
+        in_specs=[hbm, hbm, hbm, smem, hbm, hbm, hbm],
+        out_specs=(hbm, vmem),
         scratch_shapes=[
             pltpu.VMEM((slots * 4, LANES), f32),
             pltpu.VMEM((slots // LANES, LANES), i32),
             pltpu.VMEM((slots // LANES, LANES), i32),
+            pltpu.VMEM((ndev, LANES), i32),
             pltpu.VMEM((slots, 12 * LANES), bf16),
             pltpu.VMEM((ndev, PAD, LANES), f32),
             pltpu.VMEM((ndev, PAD, LANES), f32),
@@ -457,7 +480,8 @@
             pltpu.VMEM((4, LANES, rows), f32),
             pltpu.VMEM((4, LANES, rows + 2 * LANES), f32),
             pltpu.VMEM((ndev, LANES), f32),
-            dma((5,)),
+            dma((6,)),
+            dma((4,)),
             dma((chunks,)),
             dma((chunks,)),
             dma,
@@ -476,7 +500,17 @@
         counts,
         viscosity,
         friction,
+        codes,
     )
+    block = min(128, rows)
+    spec = pl.BlockSpec((2, block, columns), lambda i: (0, i, 0))
+    return pl.pallas_call(
+        combine,
+        out_shape=(out, out),
+        grid=(rows // block,),
+        in_specs=[pl.BlockSpec((8, LANES), lambda i: (0, 0)), pl.BlockSpec((4, 2, block, columns), lambda i: (0, 0, i, 0))],
+        out_specs=(spec, spec),
+    )(weights, basis)
 
 
 def solution(mesh):

time: 65 us -> 61.2 us (0.942)
  local copies, waits for them, and re-layouts: 3.32 us -> 0 us
    unnamed x4 -> x0, local copies, waits for them, and re-layouts: 3.32 us -> none
    pallas_call x1 -> x2, Pallas kernels: 60.2 us -> 59.8 us  [the longest x1 56.2 us: shards(): pl.pallas_call(functools.partial(kernel, n_gx, n_gy, chunk), out_shape=(j...]
where the time goes in v3:
time: 61.2 us; the launch traced here: 61.1 us
  Pallas kernels  59.8 us (98%)
  between operations  1.28 us (2%)
    pallas_call x1, Pallas kernels, shards(): pl.pallas_call(functools.partial(kernel, n_gx, n_gy, chunk), out_shape=(j...  56.2 us
    pallas_call x1, Pallas kernels, shards(): pl.pallas_call(combine, out_shape=(out, out), grid=(rows // block,), in_s...  3.65 us

profile of v3, /device:TPU:1, one launch (start us, length us, event | category | flops | bytes accessed | tf_op | source)
XLA Modules:
  0.0 61.1 jit_solution(11165666539059842922)
XLA Ops:
  1.3 56.2 %shard_map.86 = (f32[4,2,256,512]{3,2,1,0:T(8,128)}, f32[8,128]{1,0:T(8,128)}) custom-call(f32[4096,128]{1,0:T(8,128)} %bitcast.7, s32[8,128]{1,0:T(8,128)} %bitcast.8, s32[8,128]{1,0:T(8,128)} %bitcast.9, s32[1]{0:T(128)S(6)} %copy.10.counts, f32[256,512]{1,0:T(8,128)} %viscosity_hbm.1, f32[256,512]{1,0:T(8,128)} %friction_hbm.1, ...), custom_call_target="tpu_custom_call" | custom-call | tf_op jit(solution)/shard_map/pallas_call | solution.py:461
  57.5 3.7 %shard_map.87 = (f32[2,256,512]{2,1,0:T(8,128)}, f32[2,256,512]{2,1,0:T(8,128)}) custom-call(f32[8,128]{1,0:T(8,128)} %get-tuple-element.4.weights, f32[4,2,256,512]{3,2,1,0:T(8,128)} %get-tuple-element.5.basis), custom_call_target="tpu_custom_call" | custom-call | tf_op jit(solution)/shard_map/pallas_call | solution.py:507

commit v4 on v3

--- a/solution.py
+++ b/solution.py
@@ -64,9 +64,9 @@
 
 def kernel(
     n_gx, n_gy, chunk,
-    misfit_hbm, owners_hbm, offsets_hbm, counts, viscosity_hbm, friction_hbm, codes_hbm, basis, weights_out,
-    misfit, owners, offsets, codes, parts, send, recv, deposit, field, nodes, q1, q2, q3, strips, halo, sums,
-    in_sem, out_sem, a2a_send, a2a_recv, self_sem, ex_send, ex_recv, ar_send, ar_recv,
+    misfit_hbm, owners_hbm, offsets_hbm, counts_hbm, viscosity_hbm, friction_hbm, codes_hbm, basis, weights_out,
+    misfit, owners, offsets, codes, counts, parts, send, recv, deposit, field, nodes, halved, q1, q2, q3, strips, halo, sums,
+    in_sem, out_sem, a2a_send, a2a_recv, ex_send, ex_recv, ar_send, ar_recv,
 ):
     ndev = n_gx * n_gy
     ix, iy = lax.axis_index("gx"), lax.axis_index("gy")
@@ -97,6 +97,7 @@
                 (owners_hbm, owners),
                 (offsets_hbm, offsets),
                 (codes_hbm, codes),
+                (counts_hbm, counts),
                 (viscosity_hbm, field.at[0, pl.ds(HALO, rows), pl.ds(0, columns)]),
                 (friction_hbm, field.at[1, pl.ds(HALO, rows), pl.ds(0, columns)]),
                 (misfit_hbm, misfit),
@@ -109,10 +110,10 @@
     for shift in farthest:
         pl.semaphore_signal(barrier, inc=1, device_id=peer(shift), device_id_type=MESH)
 
-    for load in loads[:3]:
+    for load in loads[:4]:
         load.wait()
 
-    count = counts[0]
+    count = counts[...]
     lane_blocks = slots // LANES
     upper = (iota((LANES, LANES), 0) < iota((LANES, LANES), 1)).astype(bf16)
     carry = jnp.zeros((ndev, 1), f32)
@@ -140,8 +141,8 @@
     meta = lax.dot_general(hot, weight, (((1,), (1,)), ((), ())), preferred_element_type=f32)
     meta = meta[:, :LANES] * 512.0 + meta[:, LANES:]
 
-    loads[3].wait()
     loads[4].wait()
+    loads[5].wait()
 
     def share_tile(t, total):
         at = pl.ds(pl.multiple_of(t * 8 + HALO, 8), 8)
@@ -152,7 +153,7 @@
     share = jnp.round(share * (GRAIN / (rows * columns)))
     send[:, 32, :] = jnp.where(iota((ndev, LANES), 1) < 64, meta, share)
 
-    loads[5].wait()
+    loads[6].wait()
     for t in range(4):
         hi, mid, low = split3(misfit[pl.ds(t, slots, stride=4), :])
         parts[:, pl.ds(t * LANES, LANES)] = hi
@@ -184,7 +185,6 @@
     side = jnp.where(lane_tile < 64, jnp.where(ix < n_gx - 1, 1.0, 0.0), jnp.where(ix > 0, 1.0, 0.0))
     above = jnp.where(iy > 0, 1.0, 0.0)
     below = jnp.where(iy < n_gy - 1, 1.0, 0.0)
-    mask_main = jnp.concatenate([jnp.ones((8, columns), f32), side], axis=1)
 
     def copies(c):
         pair = pl.ds(c, 2)
@@ -233,7 +233,7 @@
     offer(0)
     for copy in copies(0):
         copy.start()
-    own = pltpu.make_async_copy(send.at[0, pl.ds(0, MSG), :], recv.at[0, pl.ds(0, MSG), :], self_sem)
+    own = pltpu.make_async_copy(send.at[0, pl.ds(0, MSG), :], recv.at[0, pl.ds(0, MSG), :], a2a_recv.at[0])
     own.start()
     for g in range(1, chunks):
         pack(g)
@@ -284,18 +284,19 @@
         here = field[0, tile_at(t), :]
         following = field[0, tile_at(jnp.minimum(t + 1, tiles - 1)), :]
         pair = here + south(here, following)
-        nodes[tile_at(t), :] = 0.5 * (pair + east(pair))
+        four = pair + east(pair)
+        nodes[tile_at(t), :] = 0.5 * four
+        halved[tile_at(t), :] = 0.25 * four
         return carry
 
     lax.fori_loop(0, tiles, node_tile, 0, unroll=2)
 
     lane16 = iota((16, LANES), 1) // CAP
     sub16 = iota((16, LANES), 0)
-    own.wait()
-    shift_sum = jnp.zeros((16, LANES), f32)
-    for g in range(chunks):
-        lo = 1 if g == 0 else 0
-        got = recv.at[pl.ds(g * chunk + lo, chunk - lo), pl.ds(0, MSG), :]
+    deposit[...] = jnp.zeros_like(deposit)
+
+    def gather(g, shift_sum):
+        got = recv.at[pl.ds(g * chunk, chunk), pl.ds(0, MSG), :]
         pltpu.make_async_copy(got, got, a2a_recv.at[g]).wait()
         for h in range(chunk // 16):
             base = g * chunk + h * 16
@@ -323,49 +324,58 @@
             add = jnp.dot(
                 jnp.concatenate([row_hot] * 3, axis=1), jnp.concatenate(pieces, axis=0), preferred_element_type=f32
             )
-            if g == 0 and h == 0:
-                deposit[...] = add
-            elif g < chunks - 1 or h < chunk // 16 - 1:
-                deposit[...] += add
-            else:
-                add = deposit[...] + add
-                field[2, pl.ds(HALO, rows), pl.ds(0, columns)] = add[:, :columns]
-                field[3, pl.ds(HALO, rows), pl.ds(0, columns)] = add[:, columns:]
-    if chunks * (chunk // 16) == 1:
-        field[2, pl.ds(HALO, rows), pl.ds(0, columns)] = deposit[:, :columns]
-        field[3, pl.ds(HALO, rows), pl.ds(0, columns)] = deposit[:, columns:]
-
+            deposit[...] += add
+        return shift_sum
+
+    shift_sum = lax.fori_loop(0, chunks, gather, jnp.zeros((16, LANES), f32))
+    field[2, pl.ds(HALO, rows), pl.ds(0, columns)] = deposit[:, :columns]
+    field[3, pl.ds(HALO, rows), pl.ds(0, columns)] = deposit[:, columns:]
     sigma = jnp.sum(shift_sum, axis=0, keepdims=True)[:, 64:65] * (1.0 / (ndev * GRAIN))
     offer(2)
     for copy in copies(2):
         copy.start()
-    accept(2)
 
     def fold(x):
         return sum(x[:, k * LANES:(k + 1) * LANES] for k in range(columns // LANES))
+
+    def less(t, carry):
+        field[1, tile_at(t), :] = field[1, tile_at(t), :] - sigma
+        return carry
+
+    def square(t, total):
+        u, v = field[2, tile_at(t), pl.ds(0, columns)], field[3, tile_at(t), pl.ds(0, columns)]
+        return total + fold(u * u + v * v)
+
+    for copy in copies(0):
+        copy.wait_send()
+    lax.fori_loop(0, tiles, less, 0, unroll=2)
+    first_product = lax.fori_loop(1, tiles - 1, square, jnp.zeros((8, LANES), f32), unroll=4)
+    accept(2)
 
     def apply(source, target, products):
         su, sv = source
         tu, tv = target
 
         def step(t, carry, mask, count_it):
-            syy_old, sxy_old, acc = carry
+            u, v, syy_old, sxy_old, acc = carry
             nxt = min(t + 1, tiles - 1) if isinstance(t, int) else t + 1
             here, there = tile_at(t), tile_at(nxt)
-            u, v = su[here, :], sv[here, :]
-            us, vs = south(u, su[there, :]), south(v, sv[there, :])
+            un, vn = su[there, :], sv[there, :]
+            us, vs = south(u, un), south(v, vn)
             s = nodes[here, :]
             exx = east(u) - u
             eyy = vs - v
             both = exx + eyy
             sxx = s * (exx + both)
             syy = s * (eyy + both)
-            sxy = (0.5 * s) * ((us - u) + (east(v) - v))
-            drag = field[1, here, :] - sigma
+            sxy = halved[here, :] * ((us - u) + (east(v) - v))
+            drag = field[1, here, :]
             au = (west(sxx) - sxx) + (north(sxy, sxy_old) - sxy) + drag * u
             av = (north(syy, syy_old) - syy) + (west(sxy) - sxy) + drag * v
-            au = au * mask
-            av = av * mask
+            au = jnp.concatenate([au[:, :columns], au[:, columns:] * side], axis=1)
+            av = jnp.concatenate([av[:, :columns], av[:, columns:] * side], axis=1)
+            if mask is not None:
+                au, av = au * mask, av * mask
             tu[here, :] = au
             tv[here, :] = av
             if count_it:
@@ -373,18 +383,19 @@
                     a + fold(p[0] * q[0] + p[1] * q[1])
                     for a, (p, q) in zip(acc, [(((u, v), (au, av))[i], ((u, v), (au, av))[j]) for i, j in products])
                 )
-            return syy, sxy, acc
+            return un, vn, syy, sxy, acc
 
         zero = jnp.zeros((8, width), f32)
-        carry = (zero, zero, tuple(jnp.zeros((8, LANES), f32) for _ in products))
-        carry = step(0, carry, mask_main * above, False)
-        carry = lax.fori_loop(1, tiles - 1, lambda t, c: step(t, c, mask_main, True), carry, unroll=8)
-        carry = step(tiles - 1, carry, mask_main * below, False)
-        return [jnp.sum(a, axis=0, keepdims=True) for a in carry[2]]
+        carry = (su[tile_at(0), :], sv[tile_at(0), :], zero, zero, tuple(jnp.zeros((8, LANES), f32) for _ in products))
+        carry = step(0, carry, above, False)
+        carry = lax.fori_loop(1, tiles - 1, lambda t, c: step(t, c, None, True), carry, unroll=8)
+        carry = step(tiles - 1, carry, below, False)
+        return [jnp.sum(a, axis=0, keepdims=True) for a in carry[4]]
 
     f0 = (field.at[2], field.at[3])
     f1, f2, f3 = ((q.at[0], q.at[1]) for q in (q1, q2, q3))
-    terms = apply(f0, f1, ((0, 0), (0, 1), (1, 1)))
+    terms = [jnp.sum(first_product, axis=0, keepdims=True)]
+    terms += apply(f0, f1, ((0, 1), (1, 1)))
     terms += apply(f1, f2, ((0, 1), (1, 1)))
     terms += apply(f2, f3, ((0, 1),))
     saves = [
@@ -424,9 +435,8 @@
     for save in saves:
         save.wait()
 
-    for c in (0, 2):
-        for copy in copies(c):
-            copy.wait_send()
+    for copy in copies(2):
+        copy.wait_send()
     others = sums.at[pl.ds(1, ndev - 1), :]
     pltpu.make_async_copy(others, others, ar_send).wait()
     for g in range(chunks):
@@ -453,7 +463,6 @@
     pixels = misfit.reshape(slots, 2, 2, LANES).transpose(0, 2, 1, 3).reshape(slots * 4, LANES)
     vmem = pl.BlockSpec(memory_space=pltpu.VMEM)
     hbm = pl.BlockSpec(memory_space=pltpu.HBM)
-    smem = pl.BlockSpec(memory_space=pltpu.SMEM)
     out = jax.ShapeDtypeStruct((2, rows, columns), f32)
     sizes, order, _ = plan(n_gx, n_gy)
     codes = np.tile(np.array([[code(s, sizes)] for s in order], np.int32), (1, LANES))
@@ -461,18 +470,20 @@
     basis, weights = pl.pallas_call(
         functools.partial(kernel, n_gx, n_gy, chunk),
         out_shape=(jax.ShapeDtypeStruct((4, 2, rows, columns), f32), jax.ShapeDtypeStruct((8, LANES), f32)),
-        in_specs=[hbm, hbm, hbm, smem, hbm, hbm, hbm],
+        in_specs=[hbm] * 7,
         out_specs=(hbm, vmem),
         scratch_shapes=[
             pltpu.VMEM((slots * 4, LANES), f32),
             pltpu.VMEM((slots // LANES, LANES), i32),
             pltpu.VMEM((slots // LANES, LANES), i32),
             pltpu.VMEM((ndev, LANES), i32),
+            pltpu.VMEM((1, 1), i32),
             pltpu.VMEM((slots, 12 * LANES), bf16),
             pltpu.VMEM((ndev, PAD, LANES), f32),
             pltpu.VMEM((ndev, PAD, LANES), f32),
             pltpu.VMEM((rows, 2 * columns), f32),
             pltpu.VMEM((4,) + padded, f32),
+            pltpu.VMEM(padded, f32),
             pltpu.VMEM(padded, f32),
             pltpu.VMEM((2,) + padded, f32),
             pltpu.VMEM((2,) + padded, f32),
@@ -480,11 +491,10 @@
             pltpu.VMEM((4, LANES, rows), f32),
             pltpu.VMEM((4, LANES, rows + 2 * LANES), f32),
             pltpu.VMEM((ndev, LANES), f32),
-            dma((6,)),
+            dma((7,)),
             dma((4,)),
             dma((chunks,)),
             dma((chunks,)),
-            dma,
             dma((2, 8)),
             dma((2, 8)),
             dma,
@@ -497,7 +507,7 @@
         pixels,
         owners.reshape(slots // LANES, LANES),
         offsets.reshape(slots // LANES, LANES),
-        counts,
+        counts.reshape(1, 1),
         viscosity,
         friction,
         codes,

time: 61.2 us -> 60.7 us (level)
  no operation moved by 1% of the time
where the time goes in v4:
time: 60.7 us; the launch traced here: 60.6 us
  Pallas kernels  59.3 us (98%)
  between operations  1.28 us (2%)
    pallas_call x1, Pallas kernels, shards(): pl.pallas_call(functools.partial(kernel, n_gx, n_gy, chunk), out_shape=(j...  55.6 us
    pallas_call x1, Pallas kernels, shards(): pl.pallas_call(combine, out_shape=(out, out), grid=(rows // block,), in_s...  3.65 us

profile of v4, /device:TPU:1, one launch (start us, length us, event | category | flops | bytes accessed | tf_op | source)
XLA Modules:
  0.0 60.6 jit_solution(1505732775472504590)
XLA Ops:
  1.3 55.6 %shard_map.86 = (f32[4,2,256,512]{3,2,1,0:T(8,128)}, f32[8,128]{1,0:T(8,128)}) custom-call(f32[4096,128]{1,0:T(8,128)} %bitcast.9, s32[8,128]{1,0:T(8,128)} %bitcast.10, s32[8,128]{1,0:T(8,128)} %bitcast.11, s32[1,1]{1,0:T(1,128)} %bitcast.8.counts_hbm, f32[256,512]{1,0:T(8,128)} %viscosity_hbm.1, f32[256,512]{1,0:T(8,128)} %friction_hbm.1, ...), custom_call_target="tpu_custom_call" | custom-call | tf_op jit(solution)/shard_map/pallas_call | solution.py:470
  56.9 3.7 %shard_map.87 = (f32[2,256,512]{2,1,0:T(8,128)}, f32[2,256,512]{2,1,0:T(8,128)}) custom-call(f32[8,128]{1,0:T(8,128)} %get-tuple-element.4.weights, f32[4,2,256,512]{3,2,1,0:T(8,128)} %get-tuple-element.5.basis), custom_call_target="tpu_custom_call" | custom-call | tf_op jit(solution)/shard_map/pallas_call | solution.py:517

commit v5 on v4

--- a/solution.py
+++ b/solution.py
@@ -50,7 +50,7 @@
     def hops(shift):
         return sum(min(d, n - d) for d, n in zip(shift[:-2] + shift[-1:], sizes[:-2] + sizes[-1:]))
 
-    near = sorted(shifts, key=lambda s: -hops(s))[-30 * ndev // 128:]
+    near = sorted(shifts, key=lambda s: -hops(s))[-60 * ndev // 128:]
     order = [(0,) * len(sizes)] + [s for s in shifts if s not in near] + near
     return sizes, order, sorted(shifts, key=lambda s: -hops(s))
 
@@ -331,8 +331,11 @@
     field[2, pl.ds(HALO, rows), pl.ds(0, columns)] = deposit[:, :columns]
     field[3, pl.ds(HALO, rows), pl.ds(0, columns)] = deposit[:, columns:]
     sigma = jnp.sum(shift_sum, axis=0, keepdims=True)[:, 64:65] * (1.0 / (ndev * GRAIN))
+    moves = copies(2)
+    for copy in moves[:2]:
+        copy.start()
     offer(2)
-    for copy in copies(2):
+    for copy in moves[:1:-1]:
         copy.start()
 
     def fold(x):

time: 60.7 us -> 60.6 us (level)
  no operation moved by 1% of the time
where the time goes in v5:
time: 60.6 us; the launch traced here: 60.5 us
  Pallas kernels  59.2 us (98%)
  between operations  1.28 us (2%)
    pallas_call x1, Pallas kernels, shards(): pl.pallas_call(functools.partial(kernel, n_gx, n_gy, chunk), out_shape=(j...  55.5 us
    pallas_call x1, Pallas kernels, shards(): pl.pallas_call(combine, out_shape=(out, out), grid=(rows // block,), in_s...  3.65 us

profile of v5, /device:TPU:1, one launch (start us, length us, event | category | flops | bytes accessed | tf_op | source)
XLA Modules:
  0.0 60.5 jit_solution(9025625069553516864)
XLA Ops:
  1.3 55.5 %shard_map.86 = (f32[4,2,256,512]{3,2,1,0:T(8,128)}, f32[8,128]{1,0:T(8,128)}) custom-call(f32[4096,128]{1,0:T(8,128)} %bitcast.9, s32[8,128]{1,0:T(8,128)} %bitcast.10, s32[8,128]{1,0:T(8,128)} %bitcast.11, s32[1,1]{1,0:T(1,128)} %bitcast.8.counts_hbm, f32[256,512]{1,0:T(8,128)} %viscosity_hbm.1, f32[256,512]{1,0:T(8,128)} %friction_hbm.1, ...), custom_call_target="tpu_custom_call" | custom-call | tf_op jit(solution)/shard_map/pallas_call | solution.py:473
  56.8 3.7 %shard_map.87 = (f32[2,256,512]{2,1,0:T(8,128)}, f32[2,256,512]{2,1,0:T(8,128)}) custom-call(f32[8,128]{1,0:T(8,128)} %get-tuple-element.4.weights, f32[4,2,256,512]{3,2,1,0:T(8,128)} %get-tuple-element.5.basis), custom_call_target="tpu_custom_call" | custom-call | tf_op jit(solution)/shard_map/pallas_call | solution.py:520
